TPU v7x, 512 devices: a whole 4x4x16 slice. The times are simulated.
512 devices in a mesh: ctx: 8 (over x, core), exp: 64 (over z, y).
Axes of the slice: x: 4, y: 4, z: 16, core: 2. Of those that a mesh axis runs over, the one named last changes fastest.
Arguments:
- queries: bfloat16 [64, 2, 576, 128], P('exp'), may hold values from -110 to 110
- latent_key_cache: bfloat16 [64, 576, 4096], P('exp', None, 'ctx'), may hold values from -6 to 6
- cache_lengths: int32 [64], P('exp'), may hold values from 1024 to 4096, as said below
- token_rows: bfloat16 [1024, 7168], P('exp'), may hold values from -6 to 6
- expert_ids: int32 [1024, 8], P('exp'), may hold values from 0 to 63, all different within a row; in each aligned block of 16 rows (0 to 15, 16 to 31, ...) at most 4 rows name the same one
- gate_scores: float32 [1024, 8], P('exp'), may hold values from 0.1 to 1
- up_maps: bfloat16 [64, 7168, 1024], P('exp', None, 'ctx'), may hold values from -0.0625 to 0.0625
- down_maps: bfloat16 [64, 1024, 7168], P('exp', 'ctx'), may hold values from -0.1875 to 0.1875
Outputs:
- attended: bfloat16 [64, 2, 128, 512], P('exp', None, 'ctx')
- combined: bfloat16 [1024, 7168], P('exp', 'ctx')
Inputs may be any that keep to these rules, and one draw needn't show every extreme that they name: `cache_lengths`: counts the 2 new positions; the first sequence's cache is full. `expert_ids`: each row names 8 different experts; among the rows of one index of exp no expert is named more than 4 times, and on some index some expert exactly 4 times.
All inputs are finite; a program needn't handle non-finite values.
Results may differ from a plain program's by a relative error of at most 0.0064.
Values may be sent and summed in bfloat16 or wider, within the bound.
A program may use at most 64 MiB of HBM per device.

v0:
```python
import jax
import jax.numpy as jnp
from jax import lax
from jax.sharding import PartitionSpec as P

LATENT_RANK = 512


SCALE = 192.0 ** (-0.5)
NEGATIVE = -1e30
ROUTE_SCALE = 2.5


def combined_all(value, axis, join):
    pieces = jax.tree.map(lambda part: lax.all_gather(part, axis), value)
    head = jax.tree.map(lambda part: part[0], pieces)
    tail = jax.tree.map(lambda part: part[1:], pieces)
    running, _ = lax.scan(lambda running, share: (join(running, share), None), head, tail)
    return running


def join_partials(earlier, latter):
    max_one, sum_one, val_one = earlier
    max_two, sum_two, val_two = latter
    joint_max = jnp.maximum(max_one, max_two)
    factor_one = jnp.exp(max_one - joint_max)
    factor_two = jnp.exp(max_two - joint_max)
    return (
        joint_max,
        sum_one * factor_one + sum_two * factor_two,
        val_one * factor_one[..., None] + val_two * factor_two[..., None],
    )


def send_back(expert_out):
    return lax.all_to_all(expert_out, "exp", split_axis=0, concat_axis=0, tiled=True)


def shards(
    queries,
    latent_key_cache,
    cache_lengths,
    token_rows,
    expert_ids,
    gate_scores,
    up_maps,
    down_maps,
):
    step_total = queries.shape[1]
    key_span = latent_key_cache.shape[2]
    key_start = lax.axis_index("ctx") * key_span
    positions = key_start + jnp.arange(key_span, dtype=jnp.int32)
    scores = (
        jnp.einsum("stdh,sdl->sthl", queries, latent_key_cache, preferred_element_type=jnp.float32)
        * SCALE
    )
    key_limit = (
        cache_lengths[:, None] - (step_total - 1 - jnp.arange(step_total, dtype=jnp.int32))[None, :]
    )
    live_keys = positions[None, None, None, :] < key_limit[:, :, None, None]
    block_max = jnp.max(jnp.where(live_keys, scores, NEGATIVE), axis=3)
    weights = jnp.where(live_keys, jnp.exp(scores - block_max[..., None]), 0.0)
    weight_sum = jnp.sum(weights, axis=3)
    block_value_rows = jnp.einsum(
        "sthl,sdl->sthd",
        weights.astype(jnp.bfloat16),
        latent_key_cache[:, :LATENT_RANK, :],
        preferred_element_type=jnp.float32,
    )
    head_count = queries.shape[3]
    own_heads = head_count // lax.axis_size("ctx")
    first_head = lax.axis_index("ctx") * own_heads
    joint_max, total_all, values_all = combined_all(
        (block_max, weight_sum, block_value_rows), "ctx", join_partials
    )
    total_all = lax.dynamic_slice_in_dim(total_all, first_head, own_heads, 2)
    values_all = lax.dynamic_slice_in_dim(values_all, first_head, own_heads, 2)
    attended = (values_all / total_all[..., None]).astype(jnp.bfloat16)
    rows_n, top_n = expert_ids.shape
    groups_n = lax.axis_size("exp")
    capacity = 2 * rows_n * top_n // groups_n
    slots_n = groups_n * capacity
    gate_values = (gate_scores / jnp.sum(gate_scores, axis=1, keepdims=True) * ROUTE_SCALE).astype(
        jnp.bfloat16
    )
    flat_group = expert_ids.reshape(-1)
    member = (flat_group[:, None] == jnp.arange(groups_n, dtype=jnp.int32)[None, :]).astype(
        jnp.int32
    )
    rank_in_group = jnp.sum((jnp.cumsum(member, axis=0) - 1) * member, axis=1)
    slot_index = flat_group * capacity + rank_in_group
    placed = slot_index[:, None] == jnp.arange(slots_n, dtype=jnp.int32)[None, :]
    placed_rows = placed.reshape(rows_n, top_n, slots_n).astype(jnp.bfloat16)
    outgoing = jnp.einsum("rkj,rd->jd", placed_rows, token_rows, preferred_element_type=jnp.float32)
    outgoing = outgoing.astype(jnp.bfloat16).reshape(groups_n, capacity, -1)
    inner = jnp.einsum(
        "ncd,dq->ncq",
        lax.all_to_all(outgoing, "exp", split_axis=0, concat_axis=0, tiled=True),
        up_maps[0],
        preferred_element_type=jnp.float32,
    )
    inner = jax.nn.silu(inner).astype(jnp.bfloat16)
    returned = send_back(
        jnp.einsum("ncq,qd->ncd", inner, down_maps[0], preferred_element_type=jnp.float32).astype(
            jnp.bfloat16
        )
    )
    gate_table = placed_rows * gate_values[:, :, None]
    partial_value = jnp.einsum(
        "rkj,jd->rd", gate_table, returned.reshape(slots_n, -1), preferred_element_type=jnp.float32
    )
    combined = lax.psum_scatter(partial_value, "ctx", scatter_dimension=1, tiled=True).astype(
        jnp.bfloat16
    )
    return (attended, combined)


def solution(mesh):
    in_specs = (
        P("exp", None, None, None),
        P("exp", None, "ctx"),
        P("exp"),
        P("exp", None),
        P("exp", None),
        P("exp", None),
        P("exp", None, "ctx"),
        P("exp", "ctx", None),
    )
    out_specs = (P("exp", None, "ctx", None), P("exp", "ctx"))
    return jax.shard_map(shards, mesh=mesh, in_specs=in_specs, out_specs=out_specs, check_vma=False)
```

profile of v0, /device:TPU:6, one launch (start us, length us, event | category | flops | bytes accessed | tf_op | source)
XLA Modules:
  0.0 440.5 jit_solution(11176819301621285689)
XLA Ops:
  7.2 0.0 copy-start
  7.2 0.9 copy.32
  8.1 0.1 eq.29
  8.2 0.1 fusion.31
  8.3 0.2 reduce_window_sum.11
  8.4 0.2 select_reduce_fusion.1
  8.6 0.1 reduce_sum.49
  8.7 0.7 reduce_sum.50
  9.4 0.7 multiply_convert_fusion.1
  10.1 0.1 copy.34
  10.2 0.2 convert_reduce_fusion
  10.4 3.9 fusion.35
  14.3 7.0 %reshape.132 = bf16[64,4,7168]{2,1,0:T(4,128)(2,1)} reshape(bf16[256,7168]{1,0:T(8,128)(2,1)} %fusion.35) | data formatting | bytes 7340032 | tf_op jit(solution)/shard_map/reshape | solution.py:95
  21.3 186.5 %all_to_all.10 = bf16[64,4,7168]{2,1,0:T(4,128)(2,1)} all-to-all(bf16[64,4,7168]{2,1,0:T(4,128)(2,1)} %reshape.132), channel_id=1, replica_groups=mesh['ctx'=8,'exp'=64] {'exp'}, dimensions={0} | all-to-all | bytes 7340032 | tf_op jit(solution)/shard_map/all_to_all | solution.py:98
  207.8 0.0 copy-done
  207.8 7.1 %convolution_convert_fusion = bf16[64,4,7168]{2,0,1:T(8,128)(2,1)} fusion(bf16[1,128,7168]{2,1,0:T(8,128)(2,1)S(1)} %copy-done, bf16[1,7168,128]{2,1,0:T(8,128)(2,1)} %param.16, bf16[64,4,7168]{2,1,0:T(4,128)(2,1)} %all_to_all.10), kind=kOutput, calls=%fused_computation.11 | convolution fusion | flops 941522944 | bytes 11010048 | tf_op jit(solution)/shard_map/ncq,qd->ncd/dot_general | solution.py:104
  214.9 6.7 %copy.36 = bf16[64,4,7168]{2,1,0:T(4,128)(2,1)} copy(bf16[64,4,7168]{2,0,1:T(8,128)(2,1)} %convolution_convert_fusion) | data formatting | bytes 7340032 | tf_op jit(solution)/shard_map/convert_element_type | solution.py:104
  221.6 6.2 %all-to-all-start.1 = ((bf16[64,4,7168]{2,1,0:T(4,128)(2,1)}), bf16[64,4,7168]{2,1,0:T(4,128)(2,1)}, u32[]{:S(2)}, u32[]{:S(2)}) async-start(bf16[64,4,7168]{2,1,0:T(4,128)(2,1)} %copy.36), calls=%async_computation.1 | async-start | bytes 7340032 | tf_op jit(solution)/shard_map/all_to_all | solution.py:36
  227.8 0.0 all-gather.7.cloned.1.call-start
  228.6 0.1 broadcast_compare_fusion
  228.6 0.0 copy-done.1
  228.6 0.0 copy-done.2
  228.6 0.5 select_reduce_fusion
  229.1 1.2 fusion.10
  230.3 0.0 all-gather.7.cloned.1.call-update
  230.3 0.0 reduce-scatter.2.cloned.1.call-start
  230.3 7.4 %all-gather.3 = f32[8,2,128]{2,1,0:T(2,128)S(1)} all-gather(f32[1,2,128]{2,1,0:T(2,128)S(1)} %bitcast.81), channel_id=2, replica_groups=mesh['ctx'=8,'exp'=64] {'ctx'}, dimensions={0}, use_global_device_ids=true | all-gather | bytes 9216 | tf_op jit(solution)/shard_map/all_gather | solution.py:15
  237.8 0.2 fusion.14
  238.0 10.2 %all-gather.4 = f32[8,2,128]{2,1,0:T(2,128)S(1)} all-gather(f32[1,2,128]{2,1,0:T(2,128)S(1)} %bitcast.82), channel_id=3, replica_groups=mesh['ctx'=8,'exp'=64] {'ctx'}, dimensions={0}, use_global_device_ids=true | all-gather | bytes 9216 | tf_op jit(solution)/shard_map/all_gather | solution.py:15
  248.2 21.3 %all-gather.7.cloned.1.call-done = f32[16,128,512]{2,1,0:T(8,128)} async-done(((f32[2,128,512]{2,1,0:T(8,128)}), f32[16,128,512]{2,1,0:T(8,128)}) %all-gather.7.cloned.1.call-update) | async-done | bytes 4194320 | tf_op jit(solution)/shard_map/all_gather | solution.py:15
  269.5 4.3 slice.43
  273.8 1.1 slice_bitcast_fusion
  274.9 120.0 %all-to-all-done.1 = bf16[64,4,7168]{2,1,0:T(4,128)(2,1)} async-done(((bf16[64,4,7168]{2,1,0:T(4,128)(2,1)}), bf16[64,4,7168]{2,1,0:T(4,128)(2,1)}, u32[]{:S(2)}, u32[]{:S(2)}) %all-to-all-start.1) | async-done | bytes 3670048 | tf_op jit(solution)/shard_map/all_to_all | solution.py:36
  394.9 6.7 %reshape.133 = bf16[256,7168]{1,0:T(8,128)(2,1)} reshape(bf16[64,4,7168]{2,1,0:T(4,128)(2,1)} %all-to-all-done.1) | data formatting | bytes 7340032 | tf_op jit(solution)/shard_map/reshape | solution.py:110
  401.6 3.4 fusion.34
  405.1 0.0 reduce-scatter.2.cloned.1.call-update
  405.1 9.0 %while.14 = (s32[]{:T(128)}, f32[1,2,128]{2,1,0:T(2,128)S(1)}, f32[1,2,128]{2,1,0:T(2,128)S(1)}, f32[1,2,128,512]{3,2,1,0:T(8,128)S(1)}, f32[7,1,2,128]{3,2,1,0:...) while((s32[]{:T(128)}, f32[1,2,128]{2,1,0:T(2,128)S(1)}, ...), condition=%wide.region_3.4_spmd, body=%wide.region_2.3_spmd.sunk | while | flops 395010 | bytes 1588329 | solution.py:18
  405.2 1.2 fusion.45
  406.5 1.2 fusion.45
  407.7 1.2 fusion.45
  409.0 1.2 fusion.45
  410.3 1.2 fusion.45
  411.6 1.2 fusion.45
  412.9 1.2 fusion.45
  414.1 0.1 dynamic-slice_bitcast_fusion
  414.2 0.7 divide_convert_fusion
  414.9 17.3 %reduce-scatter.2.cloned.1.call-done = f32[16,896]{1,0:T(8,128)} async-done(((f32[16,7168]{1,0:T(8,128)}), f32[16,896]{1,0:T(8,128)}) %reduce-scatter.2.cloned.1.call-update) | async-done | bytes 57360 | tf_op jit(solution)/shard_map/reduce_scatter | solution.py:112
  432.2 1.4 convert_element_type.44
  (36 shorter events, 0.3 us)
Async XLA Ops:
  7.2 200.6 %copy-start = (bf16[1,128,7168]{2,1,0:T(8,128)(2,1)S(1)}, bf16[1,128,7168]{2,1,0:T(8,128)(2,1)}, u32[]{:S(2)}) copy-start(bf16[1,128,7168]{2,1,0:T(8,128)(2,1)} %param.17) | copy-start | bytes 5505028
  221.6 7.0 %copy-start.1 = (bf16[1,576,512]{2,1,0:T(8,128)(2,1)S(1)}, bf16[1,576,512]{2,1,0:T(8,128)(2,1)}, u32[]{:S(2)}) copy-start(bf16[1,576,512]{2,1,0:T(8,128)(2,1)} %param.11) | copy-start | bytes 1769476
  221.6 7.0 %copy-start.2 = (bf16[1,2,576,128]{3,2,1,0:T(8,128)(2,1)S(1)}, bf16[1,2,576,128]{3,2,1,0:T(8,128)(2,1)}, u32[]{:S(2)}) copy-start(bf16[1,2,576,128]{3,2,1,0:T(8,128)(2,1)} %param.10) | copy-start | bytes 884740
  221.6 173.2 %all-to-all-start.1 = ((bf16[64,4,7168]{2,1,0:T(4,128)(2,1)}), bf16[64,4,7168]{2,1,0:T(4,128)(2,1)}, u32[]{:S(2)}, u32[]{:S(2)}) async-start(bf16[64,4,7168]{2,1,0:T(4,128)(2,1)} %copy.36), calls=%async_computation.1 | async-start | bytes 7340032 | tf_op jit(solution)/shard_map/all_to_all | solution.py:36
  227.8 41.6 %all-gather.7.cloned.1.call-start = ((), (), s32[]{:S(2)}) async-start(), calls=%async_computation.4 | async-start | bytes 4718592 | tf_op jit(solution)/shard_map/all_gather | solution.py:15
  230.3 201.9 %reduce-scatter.2.cloned.1.call-start = ((), (), s32[]{:S(2)}) async-start(), calls=%async_computation.3 | async-start | bytes 516096 | tf_op jit(solution)/shard_map/reduce_scatter | solution.py:112
  237.8 36.0 %copy-start.3 = (f32[8,2,128]{2,1,0:T(2,128)}, f32[8,2,128]{2,1,0:T(2,128)S(1)}, u32[]{:S(2)}) copy-start(f32[8,2,128]{2,1,0:T(2,128)S(1)} %all-gather.3) | copy-start | bytes 24580
  248.2 25.6 %copy-start.4 = (f32[8,2,128]{2,1,0:T(2,128)}, f32[8,2,128]{2,1,0:T(2,128)S(1)}, u32[]{:S(2)}) copy-start(f32[8,2,128]{2,1,0:T(2,128)S(1)} %all-gather.4) | copy-start | bytes 24580
  401.6 3.5 slice-start
  401.6 3.5 slice-start.1
Sparse Core Ops, SparseCore 0:
  230.8 38.6 all-gather.6
  405.2 26.9 reduce-scatter.1
where the time goes:
time: 445 us; the launch traced here: 441 us
  blocking collectives  204 us (46%)
  waiting for transfers between devices  159 us (36%)
  local copies, waits for them, and re-layouts  27.1 us (6%)
  matrix products  16.1 us (4%)
  between operations  14.8 us (3%)
  other arithmetic  13.2 us (3%)
  starting transfers between devices  6.28 us (1%)
    all_to_all x1, blocking collectives, shards(): lax.all_to_all(outgoing, 'exp', split_axis=0, concat_axis=0, tiled=True)  186 us
    all_to_all x1, waiting for transfers between devices, send_back(): lax.all_to_all(expert_out, 'exp', split_axis=0, concat_axis=0, tiled=True)  120 us
    all_gather x1, waiting for transfers between devices, combined_all(): pieces = jax.tree.map(lambda part: lax.all_gather(part, axis), value)  21.3 us
    all_gather x2, blocking collectives, combined_all(): pieces = jax.tree.map(lambda part: lax.all_gather(part, axis), value)  17.6 us
    reduce_scatter x1, waiting for transfers between devices, shards(): lax.psum_scatter(partial_value, 'ctx', scatter_dimension=1, tiled=True)  17.3 us
  transfers between devices with their start and end apart: 3, of which 3 were waited for; matrix products, arithmetic and copies ran while one was open for 4% of the time, Pallas kernels for 0%

commit v1 on v0

v1 whole, which is shorter than its diff:
```python
import jax
import jax.numpy as jnp
from jax import lax
from jax.sharding import PartitionSpec as P

LATENT_RANK = 512


SCALE = 192.0 ** (-0.5)
NEGATIVE = -1e30
ROUTE_SCALE = 2.5


def shards(
    queries,
    latent_key_cache,
    cache_lengths,
    token_rows,
    expert_ids,
    gate_scores,
    up_maps,
    down_maps,
):
    step_total = queries.shape[1]
    key_span = latent_key_cache.shape[2]
    key_start = lax.axis_index("ctx") * key_span
    positions = key_start + jnp.arange(key_span, dtype=jnp.int32)
    scores = (
        jnp.einsum("stdh,sdl->sthl", queries, latent_key_cache, preferred_element_type=jnp.float32)
        * SCALE
    )
    key_limit = (
        cache_lengths[:, None] - (step_total - 1 - jnp.arange(step_total, dtype=jnp.int32))[None, :]
    )
    live_keys = positions[None, None, None, :] < key_limit[:, :, None, None]
    block_max = jnp.max(jnp.where(live_keys, scores, NEGATIVE), axis=3)
    weights = jnp.where(live_keys, jnp.exp(scores - block_max[..., None]), 0.0)
    weight_sum = jnp.sum(weights, axis=3)
    block_value_rows = jnp.einsum(
        "sthl,sdl->sthd",
        weights.astype(jnp.bfloat16),
        latent_key_cache[:, :LATENT_RANK, :],
        preferred_element_type=jnp.float32,
    )
    shares_n = lax.axis_size("ctx")
    own_heads = queries.shape[3] // shares_n

    def by_heads(part):
        split = part.reshape(part.shape[:2] + (shares_n, own_heads) + part.shape[3:])
        return jnp.moveaxis(split, 2, 0)

    stats = lax.all_to_all(by_heads(jnp.stack([block_max, weight_sum], axis=-1)), "ctx", 0, 0)
    block_values = lax.all_to_all(
        by_heads(block_value_rows.astype(jnp.bfloat16)), "ctx", 0, 0
    ).astype(jnp.float32)
    factors = jnp.exp(stats[..., 0] - jnp.max(stats[..., 0], axis=0))
    total = jnp.sum(stats[..., 1] * factors, axis=0)
    attended = (
        jnp.sum(block_values * factors[..., None], axis=0) / total[..., None]
    ).astype(jnp.bfloat16)
    rows_n, top_n = expert_ids.shape
    groups_n = lax.axis_size("exp")
    capacity = 2 * rows_n * top_n // groups_n
    slots_n = groups_n * capacity
    gate_values = (gate_scores / jnp.sum(gate_scores, axis=1, keepdims=True) * ROUTE_SCALE).astype(
        jnp.bfloat16
    )
    flat_group = expert_ids.reshape(-1)
    member = (flat_group[:, None] == jnp.arange(groups_n, dtype=jnp.int32)[None, :]).astype(
        jnp.int32
    )
    rank_in_group = jnp.sum((jnp.cumsum(member, axis=0) - 1) * member, axis=1)
    slot_index = flat_group * capacity + rank_in_group
    placed = slot_index[:, None] == jnp.arange(slots_n, dtype=jnp.int32)[None, :]
    placed_rows = placed.reshape(rows_n, top_n, slots_n).astype(jnp.bfloat16)
    width = token_rows.shape[1] // shares_n
    own_columns = lax.dynamic_slice_in_dim(token_rows, lax.axis_index("ctx") * width, width, 1)
    outgoing = jnp.einsum("rkj,rd->jd", placed_rows, own_columns, preferred_element_type=jnp.float32)
    outgoing = outgoing.astype(jnp.bfloat16).reshape(groups_n, capacity, -1)
    arrived = lax.all_to_all(outgoing, "exp", split_axis=0, concat_axis=0, tiled=True)
    arrived = lax.all_gather(arrived.reshape(slots_n, width), "ctx")
    inner = jnp.einsum(
        "xjd,xdq->jq",
        arrived,
        up_maps[0].reshape(shares_n, width, -1),
        preferred_element_type=jnp.float32,
    )
    inner = jax.nn.silu(inner).astype(jnp.bfloat16)
    part_out = jnp.einsum("jq,qd->jd", inner, down_maps[0], preferred_element_type=jnp.float32)
    summed = lax.psum_scatter(
        part_out.astype(jnp.bfloat16), "ctx", scatter_dimension=1, tiled=True
    )
    returned = lax.all_to_all(
        summed.reshape(groups_n, capacity, width), "exp", split_axis=0, concat_axis=0, tiled=True
    )
    gate_table = placed_rows * gate_values[:, :, None]
    combined = jnp.einsum(
        "rkj,jd->rd", gate_table, returned.reshape(slots_n, -1), preferred_element_type=jnp.float32
    ).astype(jnp.bfloat16)
    return (attended, combined)


def solution(mesh):
    in_specs = (
        P("exp", None, None, None),
        P("exp", None, "ctx"),
        P("exp"),
        P("exp", None),
        P("exp", None),
        P("exp", None),
        P("exp", None, "ctx"),
        P("exp", "ctx", None),
    )
    out_specs = (P("exp", None, "ctx", None), P("exp", "ctx"))
    return jax.shard_map(shards, mesh=mesh, in_specs=in_specs, out_specs=out_specs, check_vma=False)
```

time: 445 us -> 204 us (0.46)
  blocking collectives: 204 us -> 48.5 us
  waiting for transfers between devices: 159 us -> 87.5 us
  starting transfers between devices: 6.28 us -> 26.7 us
  local copies, waits for them, and re-layouts: 27.1 us -> 12 us
  other arithmetic: 13.2 us -> 3.33 us
  matrix products: 16.1 us -> 9.29 us
    all_to_all x1, blocking collectives: 186 us -> 48.5 us  [shards(): lax.all_to_all(outgoing, 'exp', split_axis=0, concat_axis=0, tiled=True)]
    all_to_all x1 -> x3, waiting for transfers between devices: 120 us -> 31.8 us  [the longest x1 29.6 us: shards(): lax.all_to_all(summed.reshape(groups_n, capacity, width), 'exp', split_ax...]
    unnamed x2 -> x3, waiting for transfers between devices: 0.03 us -> 28.2 us
    all_to_all x1 -> x3, starting transfers between devices: 6.2 us -> 26.6 us  [the longest x1 15.7 us: shards(): lax.all_to_all(summed.reshape(groups_n, capacity, width), 'exp', split_ax...]
    all_gather x2 -> x0, blocking collectives: 17.6 us -> none  [combined_all(): pieces = jax.tree.map(lambda part: lax.all_gather(part, axis), value)]
    reduce_scatter x1 -> x0, waiting for transfers between devices: 17.3 us -> none  [shards(): lax.psum_scatter(partial_value, 'ctx', scatter_dimension=1, tiled=True)]
    add x7 -> x0, other arithmetic: 8.5 us -> none  [join_partials(): val_one * factor_one[..., None] + val_two * factor_two[..., None]]
    unnamed x11 -> x9, local copies, waits for them, and re-layouts: 0.92 us -> 8.24 us
  transfers between devices with their start and end apart: 3 -> 5, of which waited for: 3 -> 4; matrix products, arithmetic and copies ran while one was open for 4% -> 3% of each run, Pallas kernels for 0% -> 0%
where the time goes in v1:
time: 204 us; the launch traced here: 202 us
  waiting for transfers between devices  87.5 us (43%)
  blocking collectives  48.5 us (24%)
  starting transfers between devices  26.7 us (13%)
  between operations  14.9 us (7%)
  local copies, waits for them, and re-layouts  12 us (6%)
  matrix products  9.29 us (5%)
  other arithmetic  3.33 us (2%)
    all_to_all x1, blocking collectives, shards(): lax.all_to_all(outgoing, 'exp', split_axis=0, concat_axis=0, tiled=True)  48.5 us
    all_to_all x1, waiting for transfers between devices, shards(): lax.all_to_all(summed.reshape(groups_n, capacity, width), 'exp', split_ax...  29.6 us
    unnamed x3, waiting for transfers between devices  28.2 us
    all_gather x1, waiting for transfers between devices, shards(): arrived = lax.all_gather(arrived.reshape(slots_n, width), 'ctx')  27.5 us
    all_to_all x1, starting transfers between devices, shards(): lax.all_to_all(summed.reshape(groups_n, capacity, width), 'exp', split_ax...  15.7 us
    unnamed x9, local copies, waits for them, and re-layouts  8.24 us
    dot_general x1, matrix products, shards(): jnp.einsum('jq,qd->jd', inner, down_maps[0], preferred_element_type=jnp.f...  6.6 us
    all_to_all x1, starting transfers between devices, shards(): lax.all_to_all(by_heads(jnp.stack([block_max, weight_sum], axis=-1)), 'ct...  5.54 us
  transfers between devices with their start and end apart: 5, of which 4 were waited for; matrix products, arithmetic and copies ran while one was open for 3% of the time, Pallas kernels for 0%

profile of v1, /device:TPU:6, one launch (start us, length us, event | category | flops | bytes accessed | tf_op | source)
XLA Modules:
  0.0 202.3 jit_solution(18138412068616748986)
XLA Ops:
  7.2 0.0 copy-start
  7.2 0.0 all-gather.2.cloned.1.call-start
  7.2 0.8 reduce_sum.73
  8.1 0.7 multiply_convert_fusion.1
  8.8 0.1 copy.32
  8.8 0.8 copy.30
  9.6 0.1 eq.29
  9.7 0.1 fusion.15
  9.8 0.2 reduce_window_sum.11
  10.0 0.2 select_reduce_fusion.1
  10.1 0.1 reduce_sum.72
  10.2 0.2 convert_reduce_fusion
  10.4 1.1 convolution_convert_fusion.1
  11.5 0.1 reshape.177
  11.6 48.5 %all_to_all.20 = bf16[64,4,896]{2,1,0:T(4,128)(2,1)S(1)} all-to-all(bf16[64,4,896]{2,1,0:T(4,128)(2,1)S(1)} %reshape.177), channel_id=1, replica_groups=mesh['ctx'=8,'exp'=64] {'exp'}, dimensions={0} | all-to-all | bytes 917504 | tf_op jit(solution)/shard_map/all_to_all | solution.py:80
  60.1 0.9 all_gather_reshape.3
  61.0 0.0 all-gather.2.cloned.1.call-update
  61.0 0.0 reduce-scatter.4.cloned.1.call-start
  61.1 27.5 %all-gather.2.cloned.1.call-done = bf16[8,256,896]{2,1,0:T(8,128)(2,1)} async-done(((bf16[1,256,896]{2,1,0:T(8,128)(2,1)}), bf16[8,256,896]{2,1,0:T(8,128)(2,1)}) %all-gather.2.cloned.1.call-update) | async-done | bytes 3670032 | tf_op jit(solution)/shard_map/all_gather | solution.py:81
  88.6 0.0 copy-done
  88.6 6.6 %convolution_convert_fusion = bf16[256,7168]{1,0:T(8,128)(2,1)} fusion(bf16[1,128,7168]{2,1,0:T(8,128)(2,1)} %param.15, bf16[8,256,896]{2,1,0:T(8,128)(2,1)} %all-gather.2.cloned.1.call-done, bf16[8,896,128]{2,1,0:T(8,128)(2,1)S(1)} %bitcast.66), kind=kOutput, calls=%fused_computation | convolution fusion | flops 941522944 | bytes 11010048 | tf_op jit(solution)/shard_map/jq,qd->jd/dot_general | solution.py:89
  95.2 5.9 %copy.33 = bf16[256,7168]{0,1:T(8,128)(2,1)} copy(bf16[256,7168]{1,0:T(8,128)(2,1)} %convolution_convert_fusion) | data formatting | bytes 7340032
  101.1 0.0 copy-start.1
  101.1 0.0 copy-start.2
  101.1 0.0 reduce-scatter.4.cloned.1.call-update
  101.9 0.1 broadcast_compare_fusion
  101.9 0.2 copy-done.1
  102.2 0.1 copy-done.2
  102.2 0.5 select_reduce_fusion
  102.7 0.1 stack.9
  102.8 0.2 fusion.4
  103.0 0.1 stack.10
  103.1 0.6 copy.28
  103.7 5.5 %all-to-all-start.1 = ((f32[8,1,2,16,2]{3,2,4,1,0:T(2,128)}), f32[8,1,2,16,2]{3,2,4,1,0:T(2,128)S(1)}, u32[]{:S(2)}, u32[]{:S(2)}) async-start(f32[8,1,2,16,2]{3,2,4,1,0:T(2,128)} %copy.28), calls=%async_computation.1 | async-start | bytes 32768 | tf_op jit(solution)/shard_map/all_to_all | solution.py:52
  109.3 0.4 convolution_convert_fusion.2
  109.6 0.7 copy.37
  110.3 2.2 %all-to-all-done.1 = f32[8,1,2,16,2]{3,2,4,1,0:T(2,128)S(1)} async-done(((f32[8,1,2,16,2]{3,2,4,1,0:T(2,128)}), f32[8,1,2,16,2]{3,2,4,1,0:T(2,128)S(1)}, u32[]{:S(2)}, u32[]{:S(2)}) %all-to-all-start.1) | async-done | bytes 2080 | tf_op jit(solution)/shard_map/all_to_all | solution.py:52
  112.5 5.4 %all-to-all-start = ((bf16[8,1,2,16,512]{4,3,2,1,0:T(8,128)(2,1)}), bf16[8,1,2,16,512]{4,3,2,1,0:T(8,128)(2,1)S(1)}, u32[]{:S(2)}, u32[]{:S(2)}) async-start(bf16[8,1,2,16,512]{4,3,2,1,0:T(8,128)(2,1)} %bitcast.64), calls=%async_computation | async-start | bytes 524288 | tf_op jit(solution)/shard_map/all_to_all | solution.py:53
  118.0 28.2 %reduce-scatter.4.cloned.1.call-done = bf16[896,256]{1,0:T(8,128)(2,1)} async-done(((bf16[7168,256]{1,0:T(8,128)(2,1)}), bf16[896,256]{1,0:T(8,128)(2,1)}) %reduce-scatter.4.cloned.1.call-update) | async-done | bytes 458768
  146.2 1.3 copy.34
  147.4 0.9 reshape.178
  148.3 0.0 all-to-all-done
  148.3 15.7 %all-to-all-start.3 = ((bf16[64,4,896]{2,1,0:T(4,128)(2,1)}), bf16[64,4,896]{2,1,0:T(4,128)(2,1)S(1)}, u32[]{:S(2)}, u32[]{:S(2)}) async-start(bf16[64,4,896]{2,1,0:T(4,128)(2,1)} %reshape.178), calls=%async_computation.3 | async-start | bytes 917504 | tf_op jit(solution)/shard_map/all_to_all | solution.py:93
  164.1 0.1 multiply_reduce_fusion
  164.2 0.7 fusion.13
  164.9 29.6 %all-to-all-done.3 = bf16[64,4,896]{2,1,0:T(4,128)(2,1)S(1)} async-done(((bf16[64,4,896]{2,1,0:T(4,128)(2,1)}), bf16[64,4,896]{2,1,0:T(4,128)(2,1)S(1)}, u32[]{:S(2)}, u32[]{:S(2)}) %all-to-all-start.3) | async-done | bytes 458784 | tf_op jit(solution)/shard_map/all_to_all | solution.py:93
  194.5 0.1 reshape.179
  194.6 0.8 fusion.25
  (7 shorter events, 0.1 us)
Async XLA Ops:
  7.2 81.4 %copy-start = (bf16[1,7168,128]{2,1,0:T(8,128)(2,1)S(1)}, bf16[1,7168,128]{2,1,0:T(8,128)(2,1)}, u32[]{:S(2)}) copy-start(bf16[1,7168,128]{2,1,0:T(8,128)(2,1)} %param.14) | copy-start | bytes 5505028
  7.2 81.4 %all-gather.2.cloned.1.call-start = ((), (), s32[]{:S(2)}) async-start(), calls=%async_computation.5 | async-start | bytes 4128768 | tf_op jit(solution)/shard_map/all_gather | solution.py:81
  61.0 85.1 %reduce-scatter.4.cloned.1.call-start = ((), (), s32[]{:S(2)}) async-start(), calls=%async_computation.6 | async-start | bytes 4128768
  101.1 1.1 copy-start.1
  101.1 1.2 copy-start.2
  103.7 8.8 %all-to-all-start.1 = ((f32[8,1,2,16,2]{3,2,4,1,0:T(2,128)}), f32[8,1,2,16,2]{3,2,4,1,0:T(2,128)S(1)}, u32[]{:S(2)}, u32[]{:S(2)}) async-start(f32[8,1,2,16,2]{3,2,4,1,0:T(2,128)} %copy.28), calls=%async_computation.1 | async-start | bytes 32768 | tf_op jit(solution)/shard_map/all_to_all | solution.py:52
  112.5 35.8 %all-to-all-start = ((bf16[8,1,2,16,512]{4,3,2,1,0:T(8,128)(2,1)}), bf16[8,1,2,16,512]{4,3,2,1,0:T(8,128)(2,1)S(1)}, u32[]{:S(2)}, u32[]{:S(2)}) async-start(bf16[8,1,2,16,512]{4,3,2,1,0:T(8,128)(2,1)} %bitcast.64), calls=%async_computation | async-start | bytes 524288 | tf_op jit(solution)/shard_map/all_to_all | solution.py:53
  148.3 46.2 %all-to-all-start.3 = ((bf16[64,4,896]{2,1,0:T(4,128)(2,1)}), bf16[64,4,896]{2,1,0:T(4,128)(2,1)S(1)}, u32[]{:S(2)}, u32[]{:S(2)}) async-start(bf16[64,4,896]{2,1,0:T(4,128)(2,1)} %reshape.178), calls=%async_computation.3 | async-start | bytes 917504 | tf_op jit(solution)/shard_map/all_to_all | solution.py:93
Sparse Core Ops, SparseCore 0:
  61.2 27.3 all-gather.1
  101.2 44.9 reduce-scatter.3

commit v2 on v1

v2 whole, which is shorter than its diff:
```python
import functools

import jax
import jax.numpy as jnp
from jax import lax
from jax.experimental import pallas as pl
from jax.experimental.pallas import tpu as pltpu
from jax.sharding import PartitionSpec as P

MESH = pl.DeviceIdType.MESH
BF16, F32 = jnp.bfloat16, jnp.float32

SCALE = 192.0 ** (-0.5)
NEGATIVE = -1e30
ROUTE_SCALE = 2.5

NX, NY, NZ = 4, 4, 16
ROWS = 16
CAP = 4
WIDTH = 896
TABLE = 128
LATENT = 512
KEYS = 512
HEADS = 128
OWN_HEADS = 16
CLASSES = (0, 1, 3, 2)
SPLIT = 512
SLOTS = 4 * ROWS


def nt(a, b):
    return lax.dot_general(a, b, (((1,), (1,)), ((), ())), preferred_element_type=F32)


def tn(a, b):
    return lax.dot_general(a, b, (((0,), (0,)), ((), ())), preferred_element_type=F32)


def nn(a, b):
    return jnp.dot(a, b, preferred_element_type=F32)


def kernel(
    n_send,
    queries,
    cache,
    lengths,
    tokens,
    ids,
    gates,
    up,
    down,
    attended,
    combined,
    query_v,
    cache_v,
    up_v,
    down_v,
    rows_v,
    picked_v,
    gate_v,
    gathered_v,
    part_v,
    part_in,
    far_a,
    far_b,
    far_a_in,
    far_b_in,
    own_f,
    near_f,
    near_v,
    near_in,
    back_v,
    back_in,
    comb_v,
    comb_in,
    comb2a_in,
    comb2b_in,
    zsum,
    zfar_a,
    zfar_b,
    zfar_a_in,
    zfar_b_in,
    znear,
    znear_in,
    att_v,
    att_s,
    att_v_in,
    att_s_in,
    load_sem,
    send_sem,
    recv_sem,
):
    ctx, exp = lax.axis_index("ctx"), lax.axis_index("exp")
    x, core = ctx // 2, ctx % 2
    z, y = exp // NY, exp % NY
    sent = []

    def along_x(step):
        return (2 * ((x + step + NX) % NX) + core, exp)

    def along_y(step):
        return (ctx, NY * z + (y + step) % NY)

    def along_z(step):
        return (ctx, NY * ((z + step + NZ) % NZ) + y)

    sibling = (2 * x + 1 - core, exp)

    def send(src, dst, device):
        copy = pltpu.make_async_remote_copy(
            src_ref=src,
            dst_ref=dst,
            send_sem=send_sem.at[len(sent)],
            recv_sem=recv_sem.at[len(sent)],
            device_id=device,
            device_id_type=MESH,
        )
        copy.start()
        sent.append(copy)
        return copy

    loads = []

    def load(src, dst):
        copy = pltpu.make_async_copy(src, dst, load_sem.at[len(loads)])
        copy.start()
        loads.append(copy)
        return copy

    token_load = load(
        tokens.at[:, pl.ds(pl.multiple_of(ctx * WIDTH, 128), WIDTH)],
        rows_v.at[0, pl.ds(0, ROWS), pl.ds(0, WIDTH)],
    )
    query_load = load(queries.at[0], query_v)
    cache_load = load(cache.at[0], cache_v)
    weight_loads = []
    for r in range(NX):
        piece = pl.multiple_of((2 * ((x + r) % NX) + core) * WIDTH, 128)
        weight_loads.append(
            load(up.at[0, pl.ds(piece, WIDTH), :], up_v.at[r, :, pl.ds(0, 128)])
        )
        weight_loads.append(
            load(down.at[0, :, pl.ds(piece, WIDTH)], down_v.at[r, pl.ds(0, 128), :])
        )

    partners = [((ctx + d) % 8, exp) for d in range(1, 8)]
    partners += [along_y(d) for d in (1, 2, 3)]
    partners += [along_z(d) for d in (1, -1, 2, -2, 4, -4)]
    barrier = pltpu.get_barrier_semaphore()
    for partner in partners:
        pl.semaphore_signal(barrier, inc=1, device_id=partner, device_id_type=MESH)

    scores = gates[...]
    values = (scores / jnp.sum(scores, axis=1, keepdims=True) * ROUTE_SCALE).astype(BF16)
    values = values.astype(F32)
    chosen = ids[...]
    lane = lax.broadcasted_iota(jnp.int32, (ROWS, TABLE), 1)
    table = jnp.zeros((ROWS, TABLE), F32)
    for k in range(chosen.shape[1]):
        table = table + jnp.where(chosen[:, k : k + 1] == lane, values[:, k : k + 1], 0.0)
    rows_v[0, 0:ROWS, WIDTH:] = table.astype(BF16)
    token_load.wait()
    pl.semaphore_wait(barrier, len(partners))

    def block(c, i, lanes=None):
        i = i % 4
        if lanes is None:
            return rows_v.at[c, pl.ds(i * ROWS, ROWS), :]
        return rows_v.at[c, pl.ds(i * ROWS, ROWS), pl.ds(*lanes)]

    arrivals = {0: [], 1: [], 2: [], 3: []}

    def forward(i):
        arrivals[1].append(send(block(0, i), block(1, i), along_z(-1)))
        arrivals[3].append(send(block(0, i), block(3, i - 1), along_z(1)))
        if i in (0, 3):
            arrivals[2].append(send(block(0, i), block(2, i - 1), along_z(2)))
        if i in (0, 1):
            arrivals[2].append(send(block(0, i), block(2, i), along_z(-2)))

    from_low = send(block(0, 0), block(0, 3), along_z(4))
    from_high = send(block(0, 0), block(0, 1), along_z(-4))
    forward(0)

    weight_copies = []
    for r in range(NX):
        piece = pl.multiple_of((2 * ((x + r) % NX) + 1 - core) * WIDTH, 128)
        weight_copies.append(
            send(up.at[0, pl.ds(piece, WIDTH), :], up_v.at[r, :, pl.ds(128, 128)], sibling)
        )
        weight_copies.append(
            send(
                down.at[0, :, pl.ds(piece, WIDTH)], down_v.at[r, pl.ds(128, 128), :], sibling
            )
        )

    def attend(t):
        score = tn(query_v[t], cache_v[...]) * SCALE
        position = ctx * KEYS + lax.broadcasted_iota(jnp.int32, (HEADS, KEYS), 1)
        live = position < lengths[0] - (1 - t)
        top = jnp.max(jnp.where(live, score, NEGATIVE), axis=1, keepdims=True)
        weight = jnp.where(live, jnp.exp(score - top), 0.0)
        total = jnp.sum(weight, axis=1, keepdims=True)
        value = nt(weight.astype(BF16), cache_v[0:LATENT, :])
        att_v[t] = value.astype(BF16)
        half = lax.broadcasted_iota(jnp.int32, (HEADS, 128), 1) < 64
        att_s[t] = jnp.where(half, top, total)

    query_load.wait()
    cache_load.wait()
    attend(0)
    from_low.wait_recv()
    arrivals[0].append(send(block(0, 3, (SPLIT, 512)), block(0, 2, (SPLIT, 512)), along_z(4)))
    forward(3)
    from_high.wait_recv()
    arrivals[0].append(send(block(0, 1, (0, SPLIT)), block(0, 2, (0, SPLIT)), along_z(-4)))
    forward(1)
    attend(1)
    heads_copies = []
    for d in range(1, 8):
        other = (ctx + d) % 8
        heads = pl.ds(pl.multiple_of(other * OWN_HEADS, OWN_HEADS), OWN_HEADS)
        heads_copies.append(send(att_v.at[:, heads, :], att_v_in.at[d - 1], (other, exp)))
        heads_copies.append(send(att_s.at[:, heads, :], att_s_in.at[d - 1], (other, exp)))
    for copy in arrivals[0]:
        copy.wait_recv()
    forward(2)

    def attend_join():
        for copy in heads_copies:
            copy.wait_recv()
        heads = pl.ds(pl.multiple_of(ctx * OWN_HEADS, OWN_HEADS), OWN_HEADS)
        for t in range(2):
            stats = [att_s[t, heads, :]] + [att_s_in[d, t] for d in range(7)]
            parts = [att_v[t, heads, :]] + [att_v_in[d, t] for d in range(7)]
            top = functools.reduce(jnp.maximum, [s[:, 0:1] for s in stats])
            factors = [jnp.exp(s[:, 0:1] - top) for s in stats]
            total = sum(s[:, 64:65] * f for s, f in zip(stats, factors))
            accum = sum(p.astype(F32) * f for p, f in zip(parts, factors))
            attended[0, t] = (accum / total).astype(BF16)

    slot = lax.broadcasted_iota(jnp.int32, (SLOTS, SLOTS), 1)
    row = lax.broadcasted_iota(jnp.int32, (SLOTS, SLOTS), 0)
    same_block = (row // ROWS) == (slot % ROWS) // CAP
    slot_rank = (slot % CAP).astype(F32)
    earlier = jnp.where((row // ROWS == slot // ROWS) & (slot < row), 1.0, 0.0).astype(BF16)
    expert_lane = lax.broadcasted_iota(jnp.int32, (TABLE, SLOTS), 0)
    expert_slot = lax.broadcasted_iota(jnp.int32, (TABLE, SLOTS), 1)
    spread = jnp.where(
        expert_lane == NY * z + (y + expert_slot // ROWS) % NY, 1.0, 0.0
    ).astype(BF16)

    y_copies, x_copies, x_relays, core_copies = {}, {}, {}, {}
    far_copies, near_copies, back_copies, comb_copies = {}, {}, {}, {}

    def select(c):
        if c:
            for copy in arrivals[c]:
                copy.wait_recv()
        gate = rows_v[c, :, WIDTH:]
        named = jnp.where(gate.astype(F32) > 0, 1.0, 0.0).astype(BF16)
        rank = nn(earlier, named).astype(BF16)
        here = nn(named, spread)
        rank_here = nn(rank, spread)
        gate_here = nn(gate, spread)
        hit = (here > 0.5) & (rank_here == slot_rank) & same_block
        gate_v[c] = jnp.where(hit, gate_here, 0.0).astype(BF16)
        picked = tn(jnp.where(hit, 1.0, 0.0).astype(BF16), rows_v[c, :, 0:WIDTH]).astype(BF16)
        picked_v[c] = picked
        gathered_v[c, 0, 0:ROWS, :] = picked[0:ROWS]
        y_copies[c] = [
            send(
                picked_v.at[c, pl.ds(d * ROWS, ROWS), :],
                gathered_v.at[c, 0, pl.ds((NY - d) * ROWS, ROWS), :],
                along_y(d),
            )
            for d in (1, 2, 3)
        ]

    def gather(c):
        for copy in y_copies[c]:
            copy.wait_recv()
        x_copies[c] = (
            send(gathered_v.at[c, 0], gathered_v.at[c, 3], along_x(1)),
            send(gathered_v.at[c, 0], gathered_v.at[c, 1], along_x(-1)),
        )

    def relay(c):
        x_copies[c][0].wait_recv()
        low = send(
            gathered_v.at[c, 3, :, pl.ds(0, SPLIT)],
            gathered_v.at[c, 2, :, pl.ds(0, SPLIT)],
            along_x(1),
        )
        x_copies[c][1].wait_recv()
        high = send(
            gathered_v.at[c, 1, :, pl.ds(SPLIT, WIDTH - SPLIT)],
            gathered_v.at[c, 2, :, pl.ds(SPLIT, WIDTH - SPLIT)],
            along_x(-1),
        )
        x_relays[c] = (low, high)

    def inner_part(c):
        if c == CLASSES[0]:
            for copy in weight_loads:
                copy.wait()
            for copy in weight_copies:
                copy.wait_recv()
        part = nn(gathered_v[c, 0], up_v[0])
        part = part + nn(gathered_v[c, 1], up_v[1])
        part = part + nn(gathered_v[c, 3], up_v[3])
        for copy in x_relays[c]:
            copy.wait_recv()
        part_v[c] = part + nn(gathered_v[c, 2], up_v[2])
        core_copies[c] = send(part_v.at[c], part_in.at[c], sibling)

    def outer_part(c):
        core_copies[c].wait_recv()
        total = part_v[c] + jnp.concatenate(
            [part_in[c, :, 128:256], part_in[c, :, 0:128]], axis=1
        )
        inner = (total / (1.0 + jnp.exp(-total))).astype(BF16)
        far = nn(inner, down_v[2]).astype(BF16)
        far_a[c] = far[:, 0:SPLIT]
        far_b[c] = far[:, SPLIT:]
        far_copies[c] = (
            send(far_a.at[c], far_a_in.at[c], along_x(1)),
            send(far_b.at[c], far_b_in.at[c], along_x(-1)),
        )
        near_f[0] = nn(inner, down_v[1])
        near_f[1] = nn(inner, down_v[3])
        own_f[c] = nn(inner, down_v[0])

    def join_far(c):
        far_copies[c][0].wait_recv()
        near_v[c, 0, :, 0:SPLIT] = (near_f[0, :, 0:SPLIT] + far_a_in[c].astype(F32)).astype(BF16)
        near_v[c, 0, :, SPLIT:] = near_f[0, :, SPLIT:].astype(BF16)
        up_copy = send(near_v.at[c, 0], near_in.at[c, 0], along_x(1))
        far_copies[c][1].wait_recv()
        near_v[c, 1, :, 0:SPLIT] = near_f[1, :, 0:SPLIT].astype(BF16)
        near_v[c, 1, :, SPLIT:] = (near_f[1, :, SPLIT:] + far_b_in[c].astype(F32)).astype(BF16)
        near_copies[c] = (up_copy, send(near_v.at[c, 1], near_in.at[c, 1], along_x(-1)))

    def join_near(c):
        for copy in near_copies[c]:
            copy.wait_recv()
        total = (own_f[c] + near_in[c, 0].astype(F32) + near_in[c, 1].astype(F32)).astype(BF16)
        back_v[c] = total
        back_in[c, 0:ROWS, :] = total[0:ROWS]
        back_copies[c] = [
            send(
                back_v.at[c, pl.ds(d * ROWS, ROWS), :],
                back_in.at[c, pl.ds((NY - d) * ROWS, ROWS), :],
                along_y(d),
            )
            for d in (1, 2, 3)
        ]

    def combine(c):
        for copy in back_copies[c]:
            copy.wait_recv()
        total = nn(gate_v[c], back_in[c])
        if c == 0:
            zsum[...] = total
            return
        comb_v[c - 1] = total.astype(BF16)
        half = 2 * ROWS
        if c == 1:
            comb_copies[1] = send(comb_v.at[0], comb_in.at[0], along_z(1))
        if c == 3:
            comb_copies[3] = send(comb_v.at[2], comb_in.at[1], along_z(-1))
        if c == 2:
            comb_copies[2] = (
                send(comb_v.at[1, pl.ds(0, half), :], comb2a_in, along_z(2)),
                send(comb_v.at[1, pl.ds(half, half), :], comb2b_in, along_z(-2)),
            )

    stages = (select, gather, relay, inner_part, outer_part, join_far, join_near, combine)
    for step in range(len(CLASSES) + len(stages) - 1):
        for s in reversed(range(len(stages))):
            if 0 <= step - s < len(CLASSES):
                stages[s](CLASSES[step - s])
        if step == 2:
            attend_join()

    def place(i):
        return pl.ds((i % 4) * ROWS, ROWS)

    comb_copies[1].wait_recv()
    comb_copies[3].wait_recv()
    totals = []
    for i in range(4):
        low = comb_in[0, i * ROWS : (i + 1) * ROWS, :].astype(F32)
        j = (i + 3) % 4
        high = comb_in[1, j * ROWS : (j + 1) * ROWS, :].astype(F32)
        totals.append(zsum[i * ROWS : (i + 1) * ROWS, :] + low + high)
    across = totals[2].astype(BF16)
    zfar_a[...] = across[:, 0:SPLIT]
    zfar_b[...] = across[:, SPLIT:]
    far_up = send(zfar_a, zfar_a_in, along_z(4))
    far_down = send(zfar_b, zfar_b_in, along_z(-4))
    for copy in comb_copies[2]:
        copy.wait_recv()
    totals[0] = totals[0] + comb2a_in[0:ROWS, :].astype(F32) + comb2b_in[ROWS:, :].astype(F32)
    totals[1] = totals[1] + comb2a_in[ROWS:, :].astype(F32)
    totals[3] = totals[3] + comb2b_in[0:ROWS, :].astype(F32)
    far_up.wait_recv()
    znear[0, :, 0:SPLIT] = (totals[1][:, 0:SPLIT] + zfar_a_in[...].astype(F32)).astype(BF16)
    znear[0, :, SPLIT:] = totals[1][:, SPLIT:].astype(BF16)
    near_up = send(znear.at[0], znear_in.at[0], along_z(4))
    far_down.wait_recv()
    znear[1, :, 0:SPLIT] = totals[3][:, 0:SPLIT].astype(BF16)
    znear[1, :, SPLIT:] = (totals[3][:, SPLIT:] + zfar_b_in[...].astype(F32)).astype(BF16)
    near_down = send(znear.at[1], znear_in.at[1], along_z(-4))
    near_up.wait_recv()
    near_down.wait_recv()
    combined[...] = (totals[0] + znear_in[0].astype(F32) + znear_in[1].astype(F32)).astype(BF16)

    for copy in sent:
        copy.wait_send()
    assert len(sent) == n_send, len(sent)


N_SEND = 106


def shards(queries, cache, lengths, tokens, ids, gates, up, down):
    vmem = pl.BlockSpec(memory_space=pltpu.VMEM)
    hbm = pl.BlockSpec(memory_space=pl.ANY)
    smem = pl.BlockSpec(memory_space=pltpu.SMEM)
    n_classes = len(CLASSES)

    def buf(*shape, dtype=BF16):
        return pltpu.VMEM(shape, dtype)

    return pl.pallas_call(
        functools.partial(kernel, N_SEND),
        out_shape=(
            jax.ShapeDtypeStruct((1, 2, OWN_HEADS, LATENT), BF16),
            jax.ShapeDtypeStruct((ROWS, WIDTH), BF16),
        ),
        in_specs=[hbm, hbm, smem, hbm, vmem, vmem, hbm, hbm],
        out_specs=(vmem, vmem),
        scratch_shapes=[
            buf(2, 576, HEADS),
            buf(576, KEYS),
            buf(NX, WIDTH, 256),
            buf(NX, 256, WIDTH),
            buf(n_classes, SLOTS, WIDTH + TABLE),
            buf(n_classes, SLOTS, WIDTH),
            buf(n_classes, SLOTS, SLOTS),
            buf(n_classes, NX, SLOTS, WIDTH),
            buf(n_classes, SLOTS, 256, dtype=F32),
            buf(n_classes, SLOTS, 256, dtype=F32),
            buf(n_classes, SLOTS, SPLIT),
            buf(n_classes, SLOTS, WIDTH - SPLIT),
            buf(n_classes, SLOTS, SPLIT),
            buf(n_classes, SLOTS, WIDTH - SPLIT),
            buf(n_classes, SLOTS, WIDTH, dtype=F32),
            buf(2, SLOTS, WIDTH, dtype=F32),
            buf(n_classes, 2, SLOTS, WIDTH),
            buf(n_classes, 2, SLOTS, WIDTH),
            buf(n_classes, SLOTS, WIDTH),
            buf(n_classes, SLOTS, WIDTH),
            buf(3, SLOTS, WIDTH),
            buf(2, SLOTS, WIDTH),
            buf(2 * ROWS, WIDTH),
            buf(2 * ROWS, WIDTH),
            buf(SLOTS, WIDTH, dtype=F32),
            buf(ROWS, SPLIT),
            buf(ROWS, WIDTH - SPLIT),
            buf(ROWS, SPLIT),
            buf(ROWS, WIDTH - SPLIT),
            buf(2, ROWS, WIDTH),
            buf(2, ROWS, WIDTH),
            buf(2, HEADS, LATENT),
            buf(2, HEADS, 128, dtype=F32),
            buf(7, 2, OWN_HEADS, LATENT),
            buf(7, 2, OWN_HEADS, 128, dtype=F32),
            pltpu.SemaphoreType.DMA((11,)),
            pltpu.SemaphoreType.DMA((N_SEND,)),
            pltpu.SemaphoreType.DMA((N_SEND,)),
        ],
        compiler_params=pltpu.CompilerParams(
            collective_id=0, has_side_effects=True, vmem_limit_bytes=40 * 1024 * 1024
        ),
    )(queries, cache, lengths, tokens, ids, gates, up, down)


def solution(mesh):
    in_specs = (
        P("exp", None, None, None),
        P("exp", None, "ctx"),
        P("exp"),
        P("exp", None),
        P("exp", None),
        P("exp", None),
        P("exp", None, "ctx"),
        P("exp", "ctx", None),
    )
    out_specs = (P("exp", None, "ctx", None), P("exp", "ctx"))
    return jax.shard_map(shards, mesh=mesh, in_specs=in_specs, out_specs=out_specs, check_vma=False)
```

time: 204 us -> 100 us (0.49)
  Pallas kernels: 0 us -> 89.8 us
  waiting for transfers between devices: 87.5 us -> 0 us
  blocking collectives: 48.5 us -> 0 us
  starting transfers between devices: 26.7 us -> 0 us
  between operations: 14.9 us -> 1.29 us
  matrix products: 9.29 us -> 0 us
  other arithmetic: 3.33 us -> 0 us
  local copies, waits for them, and re-layouts: 12 us -> 8.7 us
    pallas_call x0 -> x1, Pallas kernels: none -> 89.8 us  [shards(): pl.pallas_call(functools.partial(kernel, N_SEND), out_shape=(jax.ShapeDty...]
    all_to_all x1 -> x0, blocking collectives: 48.5 us -> none  [shards(): lax.all_to_all(outgoing, 'exp', split_axis=0, concat_axis=0, tiled=True)]
    all_to_all x3 -> x0, waiting for transfers between devices: 31.8 us -> none  [the longest x1 29.6 us: shards(): lax.all_to_all(summed.reshape(groups_n, capacity, width), 'exp', split_ax...]
    unnamed x3 -> x0, waiting for transfers between devices: 28.2 us -> none
    all_gather x1 -> x0, waiting for transfers between devices: 27.5 us -> none  [shards(): arrived = lax.all_gather(arrived.reshape(slots_n, width), 'ctx')]
    all_to_all x3 -> x0, starting transfers between devices: 26.6 us -> none  [the longest x1 15.7 us: shards(): lax.all_to_all(summed.reshape(groups_n, capacity, width), 'exp', split_ax...]
    dot_general x5 -> x0, matrix products: 9.29 us -> none  [the longest x1 6.6 us: shards(): jnp.einsum('jq,qd->jd', inner, down_maps[0], preferred_element_type=jnp.f...]
    unnamed x9 -> x14, local copies, waits for them, and re-layouts: 8.24 us -> 8.7 us
  transfers between devices with their start and end apart: 5 -> 0, of which waited for: 4 -> 0; matrix products, arithmetic and copies ran while one was open for 3% -> 0% of each run, Pallas kernels for 0% -> 0%
where the time goes in v2:
time: 100 us; the launch traced here: 99.8 us
  Pallas kernels  89.8 us (90%)
  local copies, waits for them, and re-layouts  8.7 us (9%)
  between operations  1.29 us (1%)
    pallas_call x1, Pallas kernels, shards(): pl.pallas_call(functools.partial(kernel, N_SEND), out_shape=(jax.ShapeDty...  89.8 us
    unnamed x14, local copies, waits for them, and re-layouts  8.7 us

profile of v2, /device:TPU:6, one launch (start us, length us, event | category | flops | bytes accessed | tf_op | source)
XLA Modules:
  0.0 99.8 jit_solution(3625128397851116262)
XLA Ops:
  1.3 0.8 copy.10.ids
  2.0 0.8 copy.11.gates
  2.8 0.0 copy-start
  2.8 1.5 %copy-done = bf16[1,7168,128]{2,1,0:T(8,128)(2,1)S(1)} copy-done((bf16[1,7168,128]{2,1,0:T(8,128)(2,1)S(1)}, bf16[1,7168,128]{2,1,0:T(8,128)(2,1)}, u32[]{:S(2)}) %copy-start) | copy-done | bytes 1835032
  4.3 0.0 copy-start.1
  4.3 1.5 %copy-done.1 = bf16[1,128,7168]{2,1,0:T(8,128)(2,1)S(1)} copy-done((bf16[1,128,7168]{2,1,0:T(8,128)(2,1)S(1)}, bf16[1,128,7168]{2,1,0:T(8,128)(2,1)}, u32[]{:S(2)}) %copy-start.1) | copy-done | bytes 1835032
  5.8 0.0 copy-start.2
  5.8 1.1 %copy-done.2 = bf16[1,576,512]{2,1,0:T(8,128)(2,1)S(1)} copy-done((bf16[1,576,512]{2,1,0:T(8,128)(2,1)S(1)}, bf16[1,576,512]{2,1,0:T(8,128)(2,1)}, u32[]{:S(2)}) %copy-start.2) | copy-done | bytes 589848
  6.9 0.0 copy-start.3
  6.9 1.0 copy-done.3
  7.8 0.0 copy-start.4
  7.8 0.9 copy-done.4
  8.8 89.8 %shard_map.95 = (bf16[1,2,16,512]{3,2,1,0:T(8,128)(2,1)S(1)}, bf16[16,896]{1,0:T(8,128)(2,1)S(1)}) custom-call(bf16[1,2,576,128]{3,2,1,0:T(8,128)(2,1)S(1)} %copy-done.3, bf16[1,576,512]{2,1,0:T(8,128)(2,1)S(1)} %copy-done.2, s32[1]{0:T(128)S(6)} %copy.14.lengths, bf16[16,7168]{1,0:T(8,128)(2,1)S(1)} %copy-done.4, s32[16,8]{1,0:T(8,128)S(1)} %copy.10.ids, ...), custom_call_target="tpu_custom_call" | custom-call | tf_op jit(solution)/shard_map/pallas_call | solution.py:437
  98.6 0.6 copy.15
  99.2 0.6 copy.16
Async XLA Ops:
  2.8 1.5 %copy-start = (bf16[1,7168,128]{2,1,0:T(8,128)(2,1)S(1)}, bf16[1,7168,128]{2,1,0:T(8,128)(2,1)}, u32[]{:S(2)}) copy-start(bf16[1,7168,128]{2,1,0:T(8,128)(2,1)} %up.1) | copy-start | bytes 5505028
  4.3 1.5 %copy-start.1 = (bf16[1,128,7168]{2,1,0:T(8,128)(2,1)S(1)}, bf16[1,128,7168]{2,1,0:T(8,128)(2,1)}, u32[]{:S(2)}) copy-start(bf16[1,128,7168]{2,1,0:T(8,128)(2,1)} %down.1) | copy-start | bytes 5505028
  5.8 1.1 %copy-start.2 = (bf16[1,576,512]{2,1,0:T(8,128)(2,1)S(1)}, bf16[1,576,512]{2,1,0:T(8,128)(2,1)}, u32[]{:S(2)}) copy-start(bf16[1,576,512]{2,1,0:T(8,128)(2,1)} %cache.1) | copy-start | bytes 1769476
  6.9 1.0 copy-start.3
  7.8 0.9 copy-start.4

commit v3 on v2

v3 whole, which is shorter than its diff:
```python
import functools

import jax
import jax.numpy as jnp
from jax import lax
from jax.experimental import pallas as pl
from jax.experimental.pallas import tpu as pltpu
from jax.sharding import PartitionSpec as P

MESH = pl.DeviceIdType.MESH
BF16, F32 = jnp.bfloat16, jnp.float32

SCALE = 192.0 ** (-0.5)
NEGATIVE = -1e30
ROUTE_SCALE = 2.5

NX, NY, NZ = 4, 4, 16
ROWS = 16
CAP = 4
WIDTH = 896
TABLE = 128
LATENT = 512
KEYS = 512
HEADS = 128
OWN_HEADS = 16
CLASSES = (0, 1, 3, 2)
BACK = (1, 3, 2, 0)
SPLITS = {1: 512, 3: 384, 2: 512, 0: 384}
UNITS = 128
SLOTS = 4 * ROWS


def nt(a, b):
    return lax.dot_general(a, b, (((1,), (1,)), ((), ())), preferred_element_type=F32)


def tn(a, b):
    return lax.dot_general(a, b, (((0,), (0,)), ((), ())), preferred_element_type=F32)


def nn(a, b):
    return jnp.dot(a, b, preferred_element_type=F32)


def kernel(
    n_send,
    queries,
    cache,
    lengths,
    tokens,
    ids,
    gates,
    up,
    down,
    attended,
    combined,
    query_v,
    cache_v,
    up_v,
    down_v,
    rows_v,
    picked_v,
    gate_v,
    gathered_v,
    part_v,
    part_in,
    own_part,
    inner_v,
    inner_in,
    far_v,
    far_in,
    own_f,
    near_f,
    near_v,
    near_in,
    back_v,
    back_in,
    comb_v,
    comb_in,
    comb2a_in,
    comb2b_in,
    zsum,
    zsend,
    zsend_in,
    att_v,
    att_s,
    att_v_in,
    att_s_in,
    load_sem,
    send_sem,
    recv_sem,
):
    ctx, exp = lax.axis_index("ctx"), lax.axis_index("exp")
    x, core = ctx // 2, ctx % 2
    z, y = exp // NY, exp % NY
    sent = []

    def along_x(step):
        return (2 * ((x + step + NX) % NX) + core, exp)

    def along_y(step):
        return (ctx, NY * z + (y + step) % NY)

    def along_z(step):
        return (ctx, NY * ((z + step + NZ) % NZ) + y)

    sibling = (2 * x + 1 - core, exp)

    def send(src, dst, device):
        copy = pltpu.make_async_remote_copy(
            src_ref=src,
            dst_ref=dst,
            send_sem=send_sem.at[len(sent)],
            recv_sem=recv_sem.at[len(sent)],
            device_id=device,
            device_id_type=MESH,
        )
        copy.start()
        sent.append(copy)
        return copy

    loads = []

    def load(src, dst):
        copy = pltpu.make_async_copy(src, dst, load_sem.at[len(loads)])
        copy.start()
        loads.append(copy)
        return copy

    token_load = load(
        tokens.at[:, pl.ds(pl.multiple_of(ctx * WIDTH, 128), WIDTH)],
        rows_v.at[0, pl.ds(0, ROWS), pl.ds(0, WIDTH)],
    )

    partners = [along_z(d) for d in (4, -4, 8, 1, -1, 2, -2)]
    partners += [along_y(d) for d in (1, 2, 3)]
    partners += [((ctx + d) % 8, exp) for d in range(1, 8)]
    barrier = pltpu.get_barrier_semaphore()
    for partner in partners:
        pl.semaphore_signal(barrier, inc=1, device_id=partner, device_id_type=MESH)

    query_load = load(queries.at[0], query_v)
    cache_load = load(cache.at[0], cache_v)

    def up_rows(step, which):
        piece = 2 * ((x + step + NX) % NX) + (1 - core if which else core)
        return up.at[0, pl.ds(pl.multiple_of(piece * WIDTH, 128), WIDTH), :]

    def up_place(which, source):
        return up_v.at[which, :, pl.ds(source * UNITS, UNITS)]

    weight_loads = [load(up_rows(0, which), up_place(which, 0)) for which in (0, 1)]
    for r in range(NX):
        piece = pl.multiple_of((2 * ((x + r) % NX) + core) * WIDTH, 128)
        weight_loads.append(
            load(down.at[0, :, pl.ds(piece, WIDTH)], down_v.at[r, pl.ds(0, UNITS), :])
        )

    scores = gates[...]
    values = (scores / jnp.sum(scores, axis=0, keepdims=True) * ROUTE_SCALE).astype(BF16)
    values = values.astype(F32)
    chosen = ids[...]
    expert = lax.broadcasted_iota(jnp.int32, (TABLE, ROWS), 0)
    table = jnp.zeros((TABLE, ROWS), F32)
    for k in range(chosen.shape[0]):
        table = table + jnp.where(chosen[k : k + 1, :] == expert, values[k : k + 1, :], 0.0)
    unit_row = lax.broadcasted_iota(jnp.int32, (TABLE, TABLE), 0)
    unit_lane = lax.broadcasted_iota(jnp.int32, (TABLE, TABLE), 1)
    unit = jnp.where(unit_row == unit_lane, 1.0, 0.0).astype(BF16)
    rows_v[0, 0:ROWS, WIDTH:] = tn(table.astype(BF16), unit).astype(BF16)
    token_load.wait()
    pl.semaphore_wait(barrier, len(partners))

    def block(c, i):
        return rows_v.at[c, pl.ds(i % 4 * ROWS, ROWS), :]

    arrivals = {1: [], 2: [], 3: []}

    def forward(i):
        arrivals[1].append(send(block(0, i), block(1, i), along_z(-1)))
        arrivals[3].append(send(block(0, i), block(3, i - 1), along_z(1)))
        if i in (0, 3):
            arrivals[2].append(send(block(0, i), block(2, i - 1), along_z(2)))
        if i in (0, 1):
            arrivals[2].append(send(block(0, i), block(2, i), along_z(-2)))

    from_low = send(block(0, 0), block(0, 3), along_z(4))
    from_high = send(block(0, 0), block(0, 1), along_z(-4))
    from_far = send(block(0, 0), block(0, 2), along_z(8))
    forward(0)

    up_copies = []
    for step in (2, 1, -1):
        for which in (0, 1):
            up_copies.append(
                send(up_rows(step, which), up_place(which, (NX - step) % NX), along_x(step))
            )
    down_copies = []
    for r in range(NX):
        piece = pl.multiple_of((2 * ((x + r) % NX) + 1 - core) * WIDTH, 128)
        down_copies.append(
            send(
                down.at[0, :, pl.ds(piece, WIDTH)],
                down_v.at[r, pl.ds(UNITS, UNITS), :],
                sibling,
            )
        )

    def attend(t):
        score = tn(query_v[t], cache_v[...]) * SCALE
        position = ctx * KEYS + lax.broadcasted_iota(jnp.int32, (HEADS, KEYS), 1)
        live = position < lengths[0] - (1 - t)
        top = jnp.max(jnp.where(live, score, NEGATIVE), axis=1, keepdims=True)
        weight = jnp.where(live, jnp.exp(score - top), 0.0)
        total = jnp.sum(weight, axis=1, keepdims=True)
        value = nt(weight.astype(BF16), cache_v[0:LATENT, :])
        att_v[t] = value.astype(BF16)
        half = lax.broadcasted_iota(jnp.int32, (HEADS, 128), 1) < 64
        att_s[t] = jnp.where(half, top, total)

    query_load.wait()
    cache_load.wait()
    attend(0)
    from_low.wait_recv()
    forward(3)
    from_high.wait_recv()
    forward(1)
    from_far.wait_recv()
    forward(2)
    attend(1)

    heads_copies = []

    def attend_send():
        for d in range(1, 8):
            other = (ctx + d) % 8
            heads = pl.ds(pl.multiple_of(other * OWN_HEADS, OWN_HEADS), OWN_HEADS)
            heads_copies.append(send(att_v.at[:, heads, :], att_v_in.at[d - 1], (other, exp)))
            heads_copies.append(send(att_s.at[:, heads, :], att_s_in.at[d - 1], (other, exp)))

    def attend_join():
        for copy in heads_copies:
            copy.wait_recv()
        heads = pl.ds(pl.multiple_of(ctx * OWN_HEADS, OWN_HEADS), OWN_HEADS)
        for t in range(2):
            stats = [att_s[t, heads, :]] + [att_s_in[d, t] for d in range(7)]
            parts = [att_v[t, heads, :]] + [att_v_in[d, t] for d in range(7)]
            top = functools.reduce(jnp.maximum, [s[:, 0:1] for s in stats])
            factors = [jnp.exp(s[:, 0:1] - top) for s in stats]
            total = sum(s[:, 64:65] * f for s, f in zip(stats, factors))
            accum = sum(p.astype(F32) * f for p, f in zip(parts, factors))
            attended[0, t] = (accum / total).astype(BF16)

    slot = lax.broadcasted_iota(jnp.int32, (SLOTS, SLOTS), 1)
    row = lax.broadcasted_iota(jnp.int32, (SLOTS, SLOTS), 0)
    same_block = (row // ROWS) == (slot % ROWS) // CAP
    slot_rank = (slot % CAP).astype(F32)
    earlier = jnp.where((row // ROWS == slot // ROWS) & (slot < row), 1.0, 0.0).astype(BF16)
    expert_lane = lax.broadcasted_iota(jnp.int32, (TABLE, SLOTS), 0)
    expert_slot = lax.broadcasted_iota(jnp.int32, (TABLE, SLOTS), 1)
    spread = jnp.where(
        expert_lane == NY * z + (y + expert_slot // ROWS) % NY, 1.0, 0.0
    ).astype(BF16)

    y_copies, pair_copies, part_copies, inner_copies = {}, {}, {}, {}
    far_copies, near_copies, back_copies, comb_copies = {}, {}, {}, {}

    def select(c):
        if c:
            for copy in arrivals[c]:
                copy.wait_recv()
        gate = rows_v[c, :, WIDTH:]
        named = jnp.where(gate.astype(F32) > 0, 1.0, 0.0).astype(BF16)
        rank = nn(earlier, named).astype(BF16)
        here = nn(named, spread)
        rank_here = nn(rank, spread)
        gate_here = nn(gate, spread)
        hit = (here > 0.5) & (rank_here == slot_rank) & same_block
        gate_v[c] = jnp.where(hit, gate_here, 0.0).astype(BF16)
        picked = tn(jnp.where(hit, 1.0, 0.0).astype(BF16), rows_v[c, :, 0:WIDTH]).astype(BF16)
        picked_v[c] = picked
        first = BACK.index(c) * SLOTS
        gathered_v[0, first : first + ROWS, :] = picked[0:ROWS]
        y_copies[c] = [
            send(
                picked_v.at[c, pl.ds(d * ROWS, ROWS), :],
                gathered_v.at[0, pl.ds(first + (NY - d) * ROWS, ROWS), :],
                along_y(d),
            )
            for d in (1, 2, 3)
        ]

    def pair(c):
        for copy in y_copies[c]:
            copy.wait_recv()
        rows = pl.ds(BACK.index(c) * SLOTS, SLOTS)
        pair_copies[c] = send(gathered_v.at[0, rows, :], gathered_v.at[1, rows, :], sibling)

    def rows_of(b):
        return pl.ds(b * 2 * SLOTS, 2 * SLOTS)

    def inner_part(b):
        if b == 0:
            for copy in weight_loads:
                copy.wait()
            for copy in up_copies:
                copy.wait_recv()
        for c in BACK[2 * b : 2 * b + 2]:
            pair_copies[c].wait_recv()
        part = nn(gathered_v[0, rows_of(b), :], up_v[0])
        part = part + nn(gathered_v[1, rows_of(b), :], up_v[1])
        own_part[b] = part[:, 0:UNITS]
        part_copies[b] = []
        for r in (2, 1, 3):
            part_v[b, r - 1] = part[:, r * UNITS : (r + 1) * UNITS].astype(BF16)
            part_copies[b].append(send(part_v.at[b, r - 1], part_in.at[b, r - 1], along_x(r)))

    def inner_sum(b):
        for copy in part_copies[b]:
            copy.wait_recv()
        total = own_part[b] + part_in[b, 0].astype(F32)
        total = total + part_in[b, 1].astype(F32) + part_in[b, 2].astype(F32)
        inner_v[b] = (total / (1.0 + jnp.exp(-total))).astype(BF16)
        inner_copies[b] = send(inner_v.at[b], inner_in.at[b], sibling)

    def outer_part(b):
        if b == 0:
            for copy in down_copies:
                copy.wait_recv()
        inner_copies[b].wait_recv()
        inner = jnp.concatenate([inner_v[b], inner_in[b]], axis=1)
        far = nn(inner, down_v[2]).astype(BF16)
        for i, c in enumerate(BACK[2 * b : 2 * b + 2]):
            far_v[c] = far[i * SLOTS : (i + 1) * SLOTS]
            low, high = pl.ds(0, SPLITS[c]), pl.ds(SPLITS[c], WIDTH - SPLITS[c])
            far_copies[c] = (
                send(far_v.at[c, :, low], far_in.at[c, :, low], along_x(1)),
                send(far_v.at[c, :, high], far_in.at[c, :, high], along_x(-1)),
            )
        near_f[b, 0] = nn(inner, down_v[1])
        near_f[b, 1] = nn(inner, down_v[3])
        own_f[b] = nn(inner, down_v[0])

    def half_of(c):
        b, i = divmod(BACK.index(c), 2)
        return b, pl.ds(i * SLOTS, SLOTS)

    def join_far(c):
        split = SPLITS[c]
        b, rows = half_of(c)
        up_near, down_near = near_f[b, 0, rows, :], near_f[b, 1, rows, :]
        far_copies[c][0].wait_recv()
        near_v[c, 0, :, 0:split] = (
            up_near[:, 0:split] + far_in[c, :, 0:split].astype(F32)
        ).astype(BF16)
        near_v[c, 0, :, split:] = up_near[:, split:].astype(BF16)
        up_copy = send(near_v.at[c, 0], near_in.at[c, 0], along_x(1))
        far_copies[c][1].wait_recv()
        near_v[c, 1, :, 0:split] = down_near[:, 0:split].astype(BF16)
        near_v[c, 1, :, split:] = (
            down_near[:, split:] + far_in[c, :, split:].astype(F32)
        ).astype(BF16)
        near_copies[c] = (up_copy, send(near_v.at[c, 1], near_in.at[c, 1], along_x(-1)))

    def join_near(c):
        for copy in near_copies[c]:
            copy.wait_recv()
        b, rows = half_of(c)
        total = (own_f[b, rows, :] + near_in[c, 0].astype(F32) + near_in[c, 1].astype(F32)).astype(BF16)
        back_v[c] = total
        back_in[c, 0:ROWS, :] = total[0:ROWS]
        back_copies[c] = [
            send(
                back_v.at[c, pl.ds(d * ROWS, ROWS), :],
                back_in.at[c, pl.ds((NY - d) * ROWS, ROWS), :],
                along_y(d),
            )
            for d in (1, 2, 3)
        ]

    def combine(c):
        for copy in back_copies[c]:
            copy.wait_recv()
        total = nn(gate_v[c], back_in[c])
        if c == 0:
            zsum[...] = total
            return
        comb_v[c - 1] = total.astype(BF16)
        half = 2 * ROWS
        if c == 1:
            comb_copies[1] = send(comb_v.at[0], comb_in.at[0], along_z(1))
        if c == 3:
            comb_copies[3] = send(comb_v.at[2], comb_in.at[1], along_z(-1))
        if c == 2:
            comb_copies[2] = (
                send(comb_v.at[1, pl.ds(0, half), :], comb2a_in, along_z(2)),
                send(comb_v.at[1, pl.ds(half, half), :], comb2b_in, along_z(-2)),
            )

    select(0)
    select(1)
    pair(0)
    select(3)
    pair(1)
    select(2)
    pair(3)
    pair(2)
    inner_part(0)
    inner_part(1)
    attend_send()
    inner_sum(0)
    inner_sum(1)
    outer_part(0)
    outer_part(1)
    join_far(BACK[0])
    join_far(BACK[1])
    join_near(BACK[0])
    join_far(BACK[2])
    join_near(BACK[1])
    join_far(BACK[3])
    combine(BACK[0])
    attend_join()
    join_near(BACK[2])
    combine(BACK[1])
    join_near(BACK[3])
    combine(BACK[2])
    combine(BACK[3])

    comb_copies[1].wait_recv()
    comb_copies[3].wait_recv()
    totals = []
    for i in range(4):
        low = comb_in[0, i * ROWS : (i + 1) * ROWS, :].astype(F32)
        j = (i + 3) % 4
        high = comb_in[1, j * ROWS : (j + 1) * ROWS, :].astype(F32)
        totals.append(zsum[i * ROWS : (i + 1) * ROWS, :] + low + high)
    for copy in comb_copies[2]:
        copy.wait_recv()
    totals[0] = totals[0] + comb2a_in[0:ROWS, :].astype(F32) + comb2b_in[ROWS:, :].astype(F32)
    totals[1] = totals[1] + comb2a_in[ROWS:, :].astype(F32)
    totals[3] = totals[3] + comb2b_in[0:ROWS, :].astype(F32)
    last_copies = []
    for i in (2, 1, 3):
        zsend[i - 1] = totals[i].astype(BF16)
        last_copies.append(send(zsend.at[i - 1], zsend_in.at[i - 1], along_z(4 * i)))
    for copy in last_copies:
        copy.wait_recv()
    combined[...] = (
        totals[0]
        + zsend_in[0].astype(F32)
        + zsend_in[1].astype(F32)
        + zsend_in[2].astype(F32)
    ).astype(BF16)

    for copy in sent:
        copy.wait_send()
    assert len(sent) == n_send, len(sent)


N_SEND = 98


def shards(queries, cache, lengths, tokens, ids, gates, up, down):
    vmem = pl.BlockSpec(memory_space=pltpu.VMEM)
    hbm = pl.BlockSpec(memory_space=pl.ANY)
    smem = pl.BlockSpec(memory_space=pltpu.SMEM)
    n_classes = len(CLASSES)

    def buf(*shape, dtype=BF16):
        return pltpu.VMEM(shape, dtype)

    return pl.pallas_call(
        functools.partial(kernel, N_SEND),
        out_shape=(
            jax.ShapeDtypeStruct((1, 2, OWN_HEADS, LATENT), BF16),
            jax.ShapeDtypeStruct((ROWS, WIDTH), BF16),
        ),
        in_specs=[hbm, hbm, smem, hbm, vmem, vmem, hbm, hbm],
        out_specs=(vmem, vmem),
        scratch_shapes=[
            buf(2, 576, HEADS),
            buf(576, KEYS),
            buf(2, WIDTH, NX * UNITS),
            buf(NX, 256, WIDTH),
            buf(n_classes, SLOTS, WIDTH + TABLE),
            buf(n_classes, SLOTS, WIDTH),
            buf(n_classes, SLOTS, SLOTS),
            buf(2, n_classes * SLOTS, WIDTH),
            buf(2, 3, 2 * SLOTS, UNITS),
            buf(2, 3, 2 * SLOTS, UNITS),
            buf(2, 2 * SLOTS, UNITS, dtype=F32),
            buf(2, 2 * SLOTS, UNITS),
            buf(2, 2 * SLOTS, UNITS),
            buf(n_classes, SLOTS, WIDTH),
            buf(n_classes, SLOTS, WIDTH),
            buf(2, 2 * SLOTS, WIDTH, dtype=F32),
            buf(2, 2, 2 * SLOTS, WIDTH, dtype=F32),
            buf(n_classes, 2, SLOTS, WIDTH),
            buf(n_classes, 2, SLOTS, WIDTH),
            buf(n_classes, SLOTS, WIDTH),
            buf(n_classes, SLOTS, WIDTH),
            buf(3, SLOTS, WIDTH),
            buf(2, SLOTS, WIDTH),
            buf(2 * ROWS, WIDTH),
            buf(2 * ROWS, WIDTH),
            buf(SLOTS, WIDTH, dtype=F32),
            buf(3, ROWS, WIDTH),
            buf(3, ROWS, WIDTH),
            buf(2, HEADS, LATENT),
            buf(2, HEADS, 128, dtype=F32),
            buf(7, 2, OWN_HEADS, LATENT),
            buf(7, 2, OWN_HEADS, 128, dtype=F32),
            pltpu.SemaphoreType.DMA((9,)),
            pltpu.SemaphoreType.DMA((N_SEND,)),
            pltpu.SemaphoreType.DMA((N_SEND,)),
        ],
        compiler_params=pltpu.CompilerParams(
            collective_id=0, has_side_effects=True, vmem_limit_bytes=60 * 1024 * 1024
        ),
    )(queries, cache, lengths, tokens, ids.T, gates.T, up, down)


def solution(mesh):
    in_specs = (
        P("exp", None, None, None),
        P("exp", None, "ctx"),
        P("exp"),
        P("exp", None),
        P("exp", None),
        P("exp", None),
        P("exp", None, "ctx"),
        P("exp", "ctx", None),
    )
    out_specs = (P("exp", None, "ctx", None), P("exp", "ctx"))
    return jax.shard_map(shards, mesh=mesh, in_specs=in_specs, out_specs=out_specs, check_vma=False)
```

time: 100 us -> 85.8 us (0.86)
  Pallas kernels: 89.8 us -> 80.7 us
  local copies, waits for them, and re-layouts: 8.7 us -> 2.73 us
    pallas_call x1, Pallas kernels: 89.8 us -> 80.7 us  [shards(): pl.pallas_call(functools.partial(kernel, N_SEND), out_shape=(jax.ShapeDty...]
    unnamed x14 -> x2, local copies, waits for them, and re-layouts: 8.7 us -> 2.73 us
where the time goes in v3:
time: 85.8 us; the launch traced here: 84.7 us
  Pallas kernels  80.7 us (94%)
  local copies, waits for them, and re-layouts  2.73 us (3%)
  between operations  1.29 us (2%)
    pallas_call x1, Pallas kernels, shards(): pl.pallas_call(functools.partial(kernel, N_SEND), out_shape=(jax.ShapeDty...  80.7 us
    unnamed x2, local copies, waits for them, and re-layouts  2.73 us

profile of v3, /device:TPU:6, one launch (start us, length us, event | category | flops | bytes accessed | tf_op | source)
XLA Modules:
  0.0 84.7 jit_solution(11672734928570356293)
XLA Ops:
  1.3 80.7 %shard_map.95 = (bf16[1,2,16,512]{3,2,1,0:T(8,128)(2,1)}, bf16[16,896]{1,0:T(8,128)(2,1)}) custom-call(bf16[1,2,576,128]{3,2,1,0:T(8,128)(2,1)} %queries.1, bf16[1,576,512]{2,1,0:T(8,128)(2,1)} %cache.1, s32[1]{0:T(128)S(6)} %copy.12.lengths, bf16[16,7168]{1,0:T(8,128)(2,1)} %tokens.1, s32[8,16]{1,0:T(8,128)} %bitcast.2, f32[8,16]{1,0:T(8,128)} %bitcast.3, ...), custom_call_target="tpu_custom_call" | custom-call | tf_op jit(solution)/shard_map/pallas_call | solution.py:472
  82.0 1.4 %copy.13 = bf16[1,2,16,512]{3,2,1,0:T(8,128)(2,1)} copy(bf16[1,2,16,512]{3,2,1,0:T(8,128)(2,1)} %get-tuple-element.4) | data formatting | bytes 65536
  83.4 1.4 %copy.14 = bf16[16,896]{1,0:T(8,128)(2,1)} copy(bf16[16,896]{1,0:T(8,128)(2,1)} %get-tuple-element.5) | data formatting | bytes 57344

commit v4 on v3

--- a/solution.py
+++ b/solution.py
@@ -25,7 +25,8 @@
 OWN_HEADS = 16
 CLASSES = (0, 1, 3, 2)
 BACK = (1, 3, 2, 0)
-SPLITS = {1: 512, 3: 384, 2: 512, 0: 384}
+SPLITS = {1: 384, 3: 512, 2: 384, 0: 512}
+COLUMNS = {1: ((0, 896),), 3: ((0, 896),), 2: ((0, 896),), 0: ((0, 512), (512, 384))}
 UNITS = 128
 SLOTS = 4 * ROWS
 
@@ -168,26 +169,7 @@
     unit_lane = lax.broadcasted_iota(jnp.int32, (TABLE, TABLE), 1)
     unit = jnp.where(unit_row == unit_lane, 1.0, 0.0).astype(BF16)
     rows_v[0, 0:ROWS, WIDTH:] = tn(table.astype(BF16), unit).astype(BF16)
-    token_load.wait()
     pl.semaphore_wait(barrier, len(partners))
-
-    def block(c, i):
-        return rows_v.at[c, pl.ds(i % 4 * ROWS, ROWS), :]
-
-    arrivals = {1: [], 2: [], 3: []}
-
-    def forward(i):
-        arrivals[1].append(send(block(0, i), block(1, i), along_z(-1)))
-        arrivals[3].append(send(block(0, i), block(3, i - 1), along_z(1)))
-        if i in (0, 3):
-            arrivals[2].append(send(block(0, i), block(2, i - 1), along_z(2)))
-        if i in (0, 1):
-            arrivals[2].append(send(block(0, i), block(2, i), along_z(-2)))
-
-    from_low = send(block(0, 0), block(0, 3), along_z(4))
-    from_high = send(block(0, 0), block(0, 1), along_z(-4))
-    from_far = send(block(0, 0), block(0, 2), along_z(8))
-    forward(0)
 
     up_copies = []
     for step in (2, 1, -1):
@@ -206,6 +188,25 @@
             )
         )
 
+    def block(c, i):
+        return rows_v.at[c, pl.ds(i % 4 * ROWS, ROWS), :]
+
+    arrivals = {1: [], 2: [], 3: []}
+
+    def forward(i):
+        arrivals[1].append(send(block(0, i), block(1, i), along_z(-1)))
+        arrivals[3].append(send(block(0, i), block(3, i - 1), along_z(1)))
+        if i in (0, 3):
+            arrivals[2].append(send(block(0, i), block(2, i - 1), along_z(2)))
+        if i in (0, 1):
+            arrivals[2].append(send(block(0, i), block(2, i), along_z(-2)))
+
+    token_load.wait()
+    from_low = send(block(0, 0), block(0, 3), along_z(4))
+    from_high = send(block(0, 0), block(0, 1), along_z(-4))
+    from_far = send(block(0, 0), block(0, 2), along_z(8))
+    forward(0)
+
     def attend(t):
         score = tn(query_v[t], cache_v[...]) * SCALE
         position = ctx * KEYS + lax.broadcasted_iota(jnp.int32, (HEADS, KEYS), 1)
@@ -227,7 +228,6 @@
     forward(1)
     from_far.wait_recv()
     forward(2)
-    attend(1)
 
     heads_copies = []
 
@@ -349,43 +349,47 @@
         split = SPLITS[c]
         b, rows = half_of(c)
         up_near, down_near = near_f[b, 0, rows, :], near_f[b, 1, rows, :]
-        far_copies[c][0].wait_recv()
-        near_v[c, 0, :, 0:split] = (
-            up_near[:, 0:split] + far_in[c, :, 0:split].astype(F32)
-        ).astype(BF16)
+        for copy in far_copies[c]:
+            copy.wait_recv()
+        far_up, far_down = far_in[c, :, 0:split].astype(F32), far_in[c, :, split:].astype(F32)
+        near_v[c, 0, :, 0:split] = (up_near[:, 0:split] + far_up).astype(BF16)
         near_v[c, 0, :, split:] = up_near[:, split:].astype(BF16)
-        up_copy = send(near_v.at[c, 0], near_in.at[c, 0], along_x(1))
-        far_copies[c][1].wait_recv()
         near_v[c, 1, :, 0:split] = down_near[:, 0:split].astype(BF16)
-        near_v[c, 1, :, split:] = (
-            down_near[:, split:] + far_in[c, :, split:].astype(F32)
-        ).astype(BF16)
-        near_copies[c] = (up_copy, send(near_v.at[c, 1], near_in.at[c, 1], along_x(-1)))
-
-    def join_near(c):
-        for copy in near_copies[c]:
+        near_v[c, 1, :, split:] = (down_near[:, split:] + far_down).astype(BF16)
+        near_copies[c] = [
+            [
+                send(near_v.at[c, i, :, pl.ds(*part)], near_in.at[c, i, :, pl.ds(*part)], along_x(d))
+                for i, d in ((0, 1), (1, -1))
+            ]
+            for part in COLUMNS[c]
+        ]
+        back_copies[c] = []
+
+    def join_near(c, p=0):
+        for copy in near_copies[c][p]:
             copy.wait_recv()
         b, rows = half_of(c)
-        total = (own_f[b, rows, :] + near_in[c, 0].astype(F32) + near_in[c, 1].astype(F32)).astype(BF16)
-        back_v[c] = total
-        back_in[c, 0:ROWS, :] = total[0:ROWS]
-        back_copies[c] = [
-            send(
-                back_v.at[c, pl.ds(d * ROWS, ROWS), :],
-                back_in.at[c, pl.ds((NY - d) * ROWS, ROWS), :],
-                along_y(d),
-            )
-            for d in (1, 2, 3)
-        ]
+        start, count = COLUMNS[c][p]
+        part = pl.ds(start, count)
+        total = own_f[b, rows, part] + near_in[c, 0, :, part].astype(F32)
+        total = (total + near_in[c, 1, :, part].astype(F32)).astype(BF16)
+        back_v[c, :, part] = total
+        back_in[c, 0:ROWS, part] = total[0:ROWS]
+        back_copies[c].append(
+            [
+                send(
+                    back_v.at[c, pl.ds(d * ROWS, ROWS), part],
+                    back_in.at[c, pl.ds((NY - d) * ROWS, ROWS), part],
+                    along_y(d),
+                )
+                for d in (2, 1, 3)
+            ]
+        )
 
     def combine(c):
-        for copy in back_copies[c]:
-            copy.wait_recv()
-        total = nn(gate_v[c], back_in[c])
-        if c == 0:
-            zsum[...] = total
-            return
-        comb_v[c - 1] = total.astype(BF16)
+        for copy in back_copies[c][0]:
+            copy.wait_recv()
+        comb_v[c - 1] = nn(gate_v[c], back_in[c]).astype(BF16)
         half = 2 * ROWS
         if c == 1:
             comb_copies[1] = send(comb_v.at[0], comb_in.at[0], along_z(1))
@@ -397,67 +401,82 @@
                 send(comb_v.at[1, pl.ds(half, half), :], comb2b_in, along_z(-2)),
             )
 
+    def from_neighbours():
+        comb_copies[1].wait_recv()
+        comb_copies[3].wait_recv()
+        for copy in comb_copies[2]:
+            copy.wait_recv()
+        for i in range(4):
+            j = (i + 3) % 4
+            total = comb_in[0, i * ROWS : (i + 1) * ROWS, :].astype(F32)
+            total = total + comb_in[1, j * ROWS : (j + 1) * ROWS, :].astype(F32)
+            if i == 0:
+                total = total + comb2a_in[0:ROWS, :].astype(F32) + comb2b_in[ROWS:, :].astype(F32)
+            if i == 1:
+                total = total + comb2a_in[ROWS:, :].astype(F32)
+            if i == 3:
+                total = total + comb2b_in[0:ROWS, :].astype(F32)
+            zsum[i * ROWS : (i + 1) * ROWS, :] = total
+
+    last_copies = []
+
+    def join_z(p):
+        for copy in back_copies[0][p]:
+            copy.wait_recv()
+        part = pl.ds(*COLUMNS[0][p])
+        total = zsum[:, part] + nn(gate_v[0], back_in[0, :, part])
+        zsum[0:ROWS, part] = total[0:ROWS]
+        for i in (2, 1, 3):
+            zsend[i - 1, :, part] = total[i * ROWS : (i + 1) * ROWS].astype(BF16)
+            last_copies.append(
+                send(zsend.at[i - 1, :, part], zsend_in.at[i - 1, :, part], along_z(4 * i))
+            )
+
     select(0)
+    attend(1)
     select(1)
+    select(3)
     pair(0)
-    select(3)
+    select(2)
     pair(1)
-    select(2)
     pair(3)
     pair(2)
     inner_part(0)
     inner_part(1)
-    attend_send()
     inner_sum(0)
     inner_sum(1)
     outer_part(0)
     outer_part(1)
-    join_far(BACK[0])
-    join_far(BACK[1])
-    join_near(BACK[0])
-    join_far(BACK[2])
-    join_near(BACK[1])
-    join_far(BACK[3])
-    combine(BACK[0])
+    join_far(1)
+    join_far(3)
+    join_near(1)
+    join_far(2)
+    join_near(3)
+    join_far(0)
+    combine(1)
+    join_near(2)
+    combine(3)
+    join_near(0, 0)
+    combine(2)
+    join_near(0, 1)
+    attend_send()
+    from_neighbours()
+    join_z(0)
+    join_z(1)
     attend_join()
-    join_near(BACK[2])
-    combine(BACK[1])
-    join_near(BACK[3])
-    combine(BACK[2])
-    combine(BACK[3])
-
-    comb_copies[1].wait_recv()
-    comb_copies[3].wait_recv()
-    totals = []
-    for i in range(4):
-        low = comb_in[0, i * ROWS : (i + 1) * ROWS, :].astype(F32)
-        j = (i + 3) % 4
-        high = comb_in[1, j * ROWS : (j + 1) * ROWS, :].astype(F32)
-        totals.append(zsum[i * ROWS : (i + 1) * ROWS, :] + low + high)
-    for copy in comb_copies[2]:
-        copy.wait_recv()
-    totals[0] = totals[0] + comb2a_in[0:ROWS, :].astype(F32) + comb2b_in[ROWS:, :].astype(F32)
-    totals[1] = totals[1] + comb2a_in[ROWS:, :].astype(F32)
-    totals[3] = totals[3] + comb2b_in[0:ROWS, :].astype(F32)
-    last_copies = []
-    for i in (2, 1, 3):
-        zsend[i - 1] = totals[i].astype(BF16)
-        last_copies.append(send(zsend.at[i - 1], zsend_in.at[i - 1], along_z(4 * i)))
     for copy in last_copies:
         copy.wait_recv()
-    combined[...] = (
-        totals[0]
-        + zsend_in[0].astype(F32)
-        + zsend_in[1].astype(F32)
-        + zsend_in[2].astype(F32)
-    ).astype(BF16)
+    total = zsum[0:ROWS, :] + zsend_in[0].astype(F32)
+    total = total + zsend_in[1].astype(F32) + zsend_in[2].astype(F32)
+    combined[...] = total.astype(BF16)
 
     for copy in sent:
         copy.wait_send()
     assert len(sent) == n_send, len(sent)
 
 
-N_SEND = 98
+N_SEND = 106
+VMEM_LIMIT = 53 * 2**20 + 12 * 2**16
 
 
 def shards(queries, cache, lengths, tokens, ids, gates, up, down):
@@ -515,7 +534,7 @@
             pltpu.SemaphoreType.DMA((N_SEND,)),
         ],
         compiler_params=pltpu.CompilerParams(
-            collective_id=0, has_side_effects=True, vmem_limit_bytes=60 * 1024 * 1024
+            collective_id=0, has_side_effects=True, vmem_limit_bytes=VMEM_LIMIT
         ),
     )(queries, cache, lengths, tokens, ids.T, gates.T, up, down)
 

time: 85.8 us -> 83.1 us (0.969); the launches traced: 84.7 us -> 82.9 us
  Pallas kernels: 80.7 us -> 79.1 us
    pallas_call x1, Pallas kernels: 80.7 us -> 79.1 us  [shards(): pl.pallas_call(functools.partial(kernel, N_SEND), out_shape=(jax.ShapeDty...]
    unnamed x2 -> x6, local copies, waits for them, and re-layouts: 2.73 us -> 2.59 us
where the time goes in v4:
time: 83.1 us; the launch traced here: 82.9 us
  Pallas kernels  79.1 us (95%)
  local copies, waits for them, and re-layouts  2.59 us (3%)
  between operations  1.3 us (2%)
    pallas_call x1, Pallas kernels, shards(): pl.pallas_call(functools.partial(kernel, N_SEND), out_shape=(jax.ShapeDty...  79.1 us
    unnamed x6, local copies, waits for them, and re-layouts  2.59 us

profile of v4, /device:TPU:6, one launch (start us, length us, event | category | flops | bytes accessed | tf_op | source)
XLA Modules:
  0.0 82.9 jit_solution(8688952904455875122)
XLA Ops:
  1.3 0.0 copy-start
  1.3 0.7 copy-done
  2.0 0.0 copy-start.1
  2.0 0.7 copy-done.1
  2.7 79.1 %shard_map.95 = (bf16[1,2,16,512]{3,2,1,0:T(8,128)(2,1)S(1)}, bf16[16,896]{1,0:T(8,128)(2,1)S(1)}) custom-call(bf16[1,2,576,128]{3,2,1,0:T(8,128)(2,1)} %queries.1, bf16[1,576,512]{2,1,0:T(8,128)(2,1)} %cache.1, s32[1]{0:T(128)S(6)} %copy.12.lengths, bf16[16,7168]{1,0:T(8,128)(2,1)} %tokens.1, s32[8,16]{1,0:T(8,128)S(1)} %bitcast.2, f32[8,16]{1,0:T(8,128)S(1)} %bitcast.3, ...), custom_call_target="tpu_custom_call" | custom-call | tf_op jit(solution)/shard_map/pallas_call | solution.py:491
  81.7 0.6 copy.13
  82.3 0.6 copy.14
Async XLA Ops:
  1.3 0.7 copy-start
  2.0 0.7 copy-start.1

commit v5 on v4

--- a/solution.py
+++ b/solution.py
@@ -23,8 +23,8 @@
 KEYS = 512
 HEADS = 128
 OWN_HEADS = 16
-CLASSES = (0, 1, 3, 2)
-BACK = (1, 3, 2, 0)
+CLASSES = (0, 2, 1, 3)
+BACK = (2, 1, 3, 0)
 SPLITS = {1: 384, 3: 512, 2: 384, 0: 512}
 COLUMNS = {1: ((0, 896),), 3: ((0, 896),), 2: ((0, 896),), 0: ((0, 512), (512, 384))}
 UNITS = 128
@@ -148,7 +148,7 @@
         return up.at[0, pl.ds(pl.multiple_of(piece * WIDTH, 128), WIDTH), :]
 
     def up_place(which, source):
-        return up_v.at[which, :, pl.ds(source * UNITS, UNITS)]
+        return up_v.at[which, source]
 
     weight_loads = [load(up_rows(0, which), up_place(which, 0)) for which in (0, 1)]
     for r in range(NX):
@@ -307,8 +307,9 @@
                 copy.wait_recv()
         for c in BACK[2 * b : 2 * b + 2]:
             pair_copies[c].wait_recv()
-        part = nn(gathered_v[0, rows_of(b), :], up_v[0])
-        part = part + nn(gathered_v[1, rows_of(b), :], up_v[1])
+        ups = [jnp.concatenate([up_v[w, r] for r in range(NX)], axis=1) for w in (0, 1)]
+        part = nn(gathered_v[0, rows_of(b), :], ups[0])
+        part = part + nn(gathered_v[1, rows_of(b), :], ups[1])
         own_part[b] = part[:, 0:UNITS]
         part_copies[b] = []
         for r in (2, 1, 3):
@@ -323,13 +324,15 @@
         inner_v[b] = (total / (1.0 + jnp.exp(-total))).astype(BF16)
         inner_copies[b] = send(inner_v.at[b], inner_in.at[b], sibling)
 
-    def outer_part(b):
+    def outer(b, r):
+        return nn(jnp.concatenate([inner_v[b], inner_in[b]], axis=1), down_v[r])
+
+    def outer_far(b):
         if b == 0:
             for copy in down_copies:
                 copy.wait_recv()
         inner_copies[b].wait_recv()
-        inner = jnp.concatenate([inner_v[b], inner_in[b]], axis=1)
-        far = nn(inner, down_v[2]).astype(BF16)
+        far = outer(b, 2).astype(BF16)
         for i, c in enumerate(BACK[2 * b : 2 * b + 2]):
             far_v[c] = far[i * SLOTS : (i + 1) * SLOTS]
             low, high = pl.ds(0, SPLITS[c]), pl.ds(SPLITS[c], WIDTH - SPLITS[c])
@@ -337,9 +340,11 @@
                 send(far_v.at[c, :, low], far_in.at[c, :, low], along_x(1)),
                 send(far_v.at[c, :, high], far_in.at[c, :, high], along_x(-1)),
             )
-        near_f[b, 0] = nn(inner, down_v[1])
-        near_f[b, 1] = nn(inner, down_v[3])
-        own_f[b] = nn(inner, down_v[0])
+
+    def outer_near(b):
+        near_f[b, 0] = outer(b, 1)
+        near_f[b, 1] = outer(b, 3)
+        own_f[b] = outer(b, 0)
 
     def half_of(c):
         b, i = divmod(BACK.index(c), 2)
@@ -434,30 +439,32 @@
 
     select(0)
     attend(1)
+    select(2)
     select(1)
+    pair(0)
     select(3)
-    pair(0)
-    select(2)
+    pair(2)
     pair(1)
     pair(3)
-    pair(2)
     inner_part(0)
     inner_part(1)
     inner_sum(0)
+    outer_far(0)
     inner_sum(1)
-    outer_part(0)
-    outer_part(1)
+    outer_near(0)
+    outer_far(1)
+    join_far(2)
     join_far(1)
+    outer_near(1)
+    join_near(2)
     join_far(3)
     join_near(1)
-    join_far(2)
+    join_far(0)
+    combine(2)
     join_near(3)
-    join_far(0)
     combine(1)
-    join_near(2)
+    join_near(0, 0)
     combine(3)
-    join_near(0, 0)
-    combine(2)
     join_near(0, 1)
     attend_send()
     from_neighbours()
@@ -499,7 +506,7 @@
         scratch_shapes=[
             buf(2, 576, HEADS),
             buf(576, KEYS),
-            buf(2, WIDTH, NX * UNITS),
+            buf(2, NX, WIDTH, UNITS),
             buf(NX, 256, WIDTH),
             buf(n_classes, SLOTS, WIDTH + TABLE),
             buf(n_classes, SLOTS, WIDTH),

time: 83.1 us -> 80.3 us (0.966)
  Pallas kernels: 79.1 us -> 76.2 us
    pallas_call x1, Pallas kernels: 79.1 us -> 76.2 us  [shards(): pl.pallas_call(functools.partial(kernel, N_SEND), out_shape=(jax.ShapeDty...]
where the time goes in v5:
time: 80.3 us; the launch traced here: 80.1 us
  Pallas kernels  76.2 us (95%)
  local copies, waits for them, and re-layouts  2.59 us (3%)
  between operations  1.3 us (2%)
    pallas_call x1, Pallas kernels, shards(): pl.pallas_call(functools.partial(kernel, N_SEND), out_shape=(jax.ShapeDty...  76.2 us
    unnamed x6, local copies, waits for them, and re-layouts  2.59 us

profile of v5, /device:TPU:6, one launch (start us, length us, event | category | flops | bytes accessed | tf_op | source)
XLA Modules:
  0.0 80.1 jit_solution(10381265696746011153)
XLA Ops:
  1.3 0.0 copy-start
  1.3 0.7 copy-done
  2.0 0.0 copy-start.1
  2.0 0.7 copy-done.1
  2.7 76.2 %shard_map.95 = (bf16[1,2,16,512]{3,2,1,0:T(8,128)(2,1)S(1)}, bf16[16,896]{1,0:T(8,128)(2,1)S(1)}) custom-call(bf16[1,2,576,128]{3,2,1,0:T(8,128)(2,1)} %queries.1, bf16[1,576,512]{2,1,0:T(8,128)(2,1)} %cache.1, s32[1]{0:T(128)S(6)} %copy.12.lengths, bf16[16,7168]{1,0:T(8,128)(2,1)} %tokens.1, s32[8,16]{1,0:T(8,128)S(1)} %bitcast.2, f32[8,16]{1,0:T(8,128)S(1)} %bitcast.3, ...), custom_call_target="tpu_custom_call" | custom-call | tf_op jit(solution)/shard_map/pallas_call | solution.py:498
  78.9 0.6 copy.13
  79.5 0.6 copy.14
Async XLA Ops:
  1.3 0.7 copy-start
  2.0 0.7 copy-start.1

commit v6 on v5

--- a/solution.py
+++ b/solution.py
@@ -202,9 +202,9 @@
             arrivals[2].append(send(block(0, i), block(2, i), along_z(-2)))
 
     token_load.wait()
+    from_far = send(block(0, 0), block(0, 2), along_z(8))
     from_low = send(block(0, 0), block(0, 3), along_z(4))
     from_high = send(block(0, 0), block(0, 1), along_z(-4))
-    from_far = send(block(0, 0), block(0, 2), along_z(8))
     forward(0)
 
     def attend(t):
@@ -451,8 +451,8 @@
     inner_sum(0)
     outer_far(0)
     inner_sum(1)
+    outer_far(1)
     outer_near(0)
-    outer_far(1)
     join_far(2)
     join_far(1)
     outer_near(1)

time: 80.3 us -> 79.5 us (0.990)
  Pallas kernels: 76.2 us -> 74.9 us
    pallas_call x1, Pallas kernels: 76.2 us -> 74.9 us  [shards(): pl.pallas_call(functools.partial(kernel, N_SEND), out_shape=(jax.ShapeDty...]
where the time goes in v6:
time: 79.5 us; the launch traced here: 78.8 us
  Pallas kernels  74.9 us (94%)
  local copies, waits for them, and re-layouts  2.59 us (3%)
  between operations  1.3 us (2%)
    pallas_call x1, Pallas kernels, shards(): pl.pallas_call(functools.partial(kernel, N_SEND), out_shape=(jax.ShapeDty...  74.9 us
    unnamed x6, local copies, waits for them, and re-layouts  2.59 us

profile of v6, /device:TPU:6, one launch (start us, length us, event | category | flops | bytes accessed | tf_op | source)
XLA Modules:
  0.0 78.8 jit_solution(17093798634792470811)
XLA Ops:
  1.3 0.0 copy-start
  1.3 0.7 copy-done
  2.0 0.0 copy-start.1
  2.0 0.7 copy-done.1
  2.7 74.9 %shard_map.95 = (bf16[1,2,16,512]{3,2,1,0:T(8,128)(2,1)S(1)}, bf16[16,896]{1,0:T(8,128)(2,1)S(1)}) custom-call(bf16[1,2,576,128]{3,2,1,0:T(8,128)(2,1)} %queries.1, bf16[1,576,512]{2,1,0:T(8,128)(2,1)} %cache.1, s32[1]{0:T(128)S(6)} %copy.12.lengths, bf16[16,7168]{1,0:T(8,128)(2,1)} %tokens.1, s32[8,16]{1,0:T(8,128)S(1)} %bitcast.2, f32[8,16]{1,0:T(8,128)S(1)} %bitcast.3, ...), custom_call_target="tpu_custom_call" | custom-call | tf_op jit(solution)/shard_map/pallas_call | solution.py:498
  77.6 0.6 copy.13
  78.2 0.6 copy.14
Async XLA Ops:
  1.3 0.7 copy-start
  2.0 0.7 copy-start.1
